TPU v7x, 32 devices: a whole 2x2x4 slice. The times are simulated.
32 devices in a mesh: wide: 8 (over z, y), narrow: 4 (over x, core).
Axes of the slice: x: 2, y: 2, z: 4, core: 2. Of those that a mesh axis runs over, the one named last changes fastest.
Arguments:
- tokens: bfloat16 [32768, 768], P(('wide', 'narrow')), may hold values from -6 to 6
- noise_mask: int32 [32768], P(('wide', 'narrow')), may hold values 0 or 1
- block_shift: int32 [32], P(('wide', 'narrow')), may hold values from 2 to 4
- cotangent: bfloat16 [32768, 768], P(('wide', 'narrow')), may hold values from -6 to 6
- input_weight: float32 [768, 2304], P('narrow'), may hold values from -0.21875 to 0.21875
- input_moment: float32 [768, 2304], P('narrow'), may hold values from -0.00048828125 to 0.00048828125
- input_square: float32 [768, 2304], P('narrow'), may hold values from 9.889956e-11 to 3.9559825e-10
- output_weight: float32 [768, 768], P('narrow'), may hold values from -0.875 to 0.875
- output_moment: float32 [768, 768], P('narrow'), may hold values from -0.00015258789 to 0.00015258789
- output_square: float32 [768, 768], P('narrow'), may hold values from 9.889956e-12 to 3.9559824e-11
- up_weight: float32 [768, 3072], P('narrow'), may hold values from -0.21875 to 0.21875
- up_moment: float32 [768, 3072], P('narrow'), may hold values from -0.00048828125 to 0.00048828125
- up_square: float32 [768, 3072], P('narrow'), may hold values from 1.13028066e-10 to 4.5211226e-10
- down_weight: float32 [3072, 768], P('narrow'), may hold values from -0.109375 to 0.109375
- down_moment: float32 [3072, 768], P('narrow'), may hold values from -0.0009765625 to 0.0009765625
- down_square: float32 [3072, 768], P('narrow'), may hold values from 4.2385526e-10 to 1.695421e-09
- up_bias: float32 [3072], P('narrow'), may hold values from -2 to 2.5
- bias_moment: float32 [3072], P('narrow'), may hold values from -0.00061035156 to 0.00061035156
- bias_square: float32 [3072], P('narrow'), may hold values from 1.4128508e-10 to 5.651403e-10
- vectors: float32 [6, 768], P(None, 'narrow'), may hold values from -4 to 4
- vector_moment: float32 [6, 768], P(None, 'narrow'), may hold values from -0.0008544922 to 0.0008544922
- vector_square: float32 [6, 768], P(None, 'narrow'), may hold values from 2.8257016e-10 to 1.1302806e-09
Outputs:
- grad_norm: float32 [1], replicated
- token_grad: float32 [32768, 768], P(('wide', 'narrow'))
- input_first: float32 [768, 2304], P('narrow')
- input_second: float32 [768, 2304], P('narrow')
- input_master: float32 [768, 2304], P('narrow')
- output_first: float32 [768, 768], P('narrow')
- output_second: float32 [768, 768], P('narrow')
- output_master: float32 [768, 768], P('narrow')
- up_first: float32 [768, 3072], P('narrow')
- up_second: float32 [768, 3072], P('narrow')
- up_master: float32 [768, 3072], P('narrow')
- down_first: float32 [3072, 768], P('narrow')
- down_second: float32 [3072, 768], P('narrow')
- down_master: float32 [3072, 768], P('narrow')
- bias_first: float32 [3072], P('narrow')
- bias_second: float32 [3072], P('narrow')
- bias_master: float32 [3072], P('narrow')
- vector_first: float32 [6, 768], P(None, 'narrow')
- vector_second: float32 [6, 768], P(None, 'narrow')
- vector_master: float32 [6, 768], P(None, 'narrow')
All inputs are finite; a program needn't handle non-finite values. No bound on the sum of `noise_mask` on one device may be relied on, other than what follows from the above.
Results may differ from a plain program's by a relative error of at most 0.018.
Values may be sent and summed in bfloat16 or wider, within the bound.
A program may use at most 512 MiB of HBM per device.

v0:
```python
import functools

import jax
import jax.numpy as jnp
import numpy as np
from jax import lax
from jax.experimental import pallas as pl
from jax.experimental.pallas import tpu as pltpu
from jax.sharding import PartitionSpec as P

D = 768
HEAD_DIM = 64
ADAM_STEP = 10
NEG_FILL = -1e30
NORM_EPS = 1e-05
BETA_ONE = 0.9
BETA_TWO = 0.999
ADAM_EPS = 1e-08
MATRIX_RATE = 0.1
VECTOR_RATE = 0.5
MATRIX_DECAY = 0.1
CLIP_LIMIT = 1.0
QUAD = 256
TILE = 256
LOG2E = 1.4426950408889634
SCORE_SCALE = HEAD_DIM**-0.5
BF = jnp.bfloat16
F32 = jnp.float32
VMEM_LIMIT = 56 * 1024 * 1024


def params(n_axes=1):
    return pltpu.CompilerParams(
        dimension_semantics=("arbitrary",) * n_axes, vmem_limit_bytes=VMEM_LIMIT
    )


def whole(shape):
    return pl.BlockSpec(shape, lambda *_: (0,) * len(shape))


def dot(a, b):
    return jnp.dot(a, b, preferred_element_type=F32)


def dot_t(a, b):
    return lax.dot_general(a, b, (((1,), (1,)), ((), ())), preferred_element_type=F32)


def t_dot(a, b):
    return lax.dot_general(a, b, (((0,), (0,)), ((), ())), preferred_element_type=F32)


def half_swap(block):
    lane = lax.broadcasted_iota(jnp.int32, block.shape, 1)
    return jnp.where(
        (lane & 63) < 32, pltpu.roll(block, 96, 1), pltpu.roll(block, 32, 1)
    )


def turn(block, cos, sin):
    return block * cos + half_swap(block) * sin


def norm_rows(rows):
    average = jnp.mean(rows, -1, keepdims=True)
    centred = rows - average
    variance = jnp.mean(centred * centred, -1, keepdims=True)
    scale = lax.rsqrt(variance + NORM_EPS)
    return centred * scale, scale


def project_kernel(
    tok, msk, vec, w, cos, sin, n1, q, kc, kn, vc, vn, nmt, held, *, tile
):
    gain, shift = 1.0 + vec[0:1, :], vec[1:2, :]

    @pl.when(pl.program_id(0) == 0)
    def _():
        x_m, _ = norm_rows(vec[5:6, :])
        n_m = (x_m * gain + shift).astype(BF)
        wide = jnp.broadcast_to(n_m.astype(F32), (128, D))
        nmt[...] = wide.T
        held[...] = dot(wide[:16].astype(BF), w[...])

    x, _ = norm_rows(tok[...].astype(F32))
    n = (x * gain + shift).astype(BF)
    n1[...] = n
    masked = jnp.broadcast_to(msk[...], (tile, 128)) > 0.5
    c, s = cos[...], sin[...]
    for j in range(3 * D // 256):
        p = dot(n, w[:, j * 256 : (j + 1) * 256])
        for i in range(2):
            col = j * 256 + i * 128
            lanes = pl.ds(col % D, 128)
            clean = p[:, i * 128 : (i + 1) * 128]
            row = jnp.broadcast_to(held[0:1, col : col + 128], (tile, 128))
            if col < D:
                q[:, lanes] = jnp.where(masked, turn(row, c, s), turn(clean, c, s)).astype(BF)
            elif col < 2 * D:
                clean = turn(clean, c, s)
                kc[:, lanes] = clean.astype(BF)
                kn[:, lanes] = jnp.where(masked, turn(row, c, s), clean).astype(BF)
            else:
                vc[:, lanes] = clean.astype(BF)
                vn[:, lanes] = jnp.where(masked, row, clean).astype(BF)


def project(tokens, mask_col, vec, w, cos, sin):
    length = tokens.shape[0]
    tile = TILE
    rows = pl.BlockSpec((tile, D), lambda i: (i, 0))
    table = pl.BlockSpec((tile, 128), lambda i: (i, 0))
    return pl.pallas_call(
        functools.partial(project_kernel, tile=tile),
        grid=(length // tile,),
        in_specs=[
            rows,
            pl.BlockSpec((tile, 1), lambda i: (i, 0)),
            whole(vec.shape),
            whole(w.shape),
            table,
            table,
        ],
        out_specs=[rows] * 6 + [whole((D, 128))],
        out_shape=[jax.ShapeDtypeStruct((length, D), BF)] * 6
        + [jax.ShapeDtypeStruct((D, 128), F32)],
        scratch_shapes=[pltpu.VMEM((16, 3 * D), F32)],
        compiler_params=params(),
        name="project",
    )(tokens, mask_col, vec, w, cos, sin)


def head_rows():
    lane = lax.broadcasted_iota(jnp.int32, (1, QUAD), 1)
    return [(lane // HEAD_DIM == h) for h in range(4)]


def stack_heads(rows, hm):
    return jnp.concatenate([rows * m.astype(BF) for m in hm], 0)


def unstack_heads(stacked, hm):
    total = None
    for h, m in enumerate(hm):
        part = jnp.where(m, stacked[h * TILE : (h + 1) * TILE], 0.0)
        total = part if total is None else total + part
    return total


def attend_kernel(shift, q, kc, kn, vc, vn, o, lse, *, length):
    hm = head_rows()
    sh = shift[0]
    rb = lax.broadcasted_iota(jnp.int32, (TILE, TILE), 0) >> sh
    cb = lax.broadcasted_iota(jnp.int32, (TILE, TILE), 1) >> sh
    same, earlier = rb == cb, cb < rb
    scale = SCORE_SCALE * LOG2E
    lane = lax.broadcasted_iota(jnp.int32, (TILE, 128), 1)
    for qt in range(length // TILE):
        here = slice(qt * TILE, (qt + 1) * TILE)
        qs = stack_heads(q[here, :], hm)
        s_c = dot_t(qs, kc[here, :])
        s_n = dot_t(qs, kn[here, :])
        if qt:
            s_f = dot_t(qs, kc[: qt * TILE, :])
        p_full, p_same, p_earl, recips = [], [], [], []
        logs = jnp.zeros((TILE, 128), F32)
        for h in range(4):
            rows = slice(h * TILE, (h + 1) * TILE)
            s_d = jnp.where(same, s_n[rows], jnp.where(earlier, s_c[rows], NEG_FILL))
            peak = jnp.max(s_d, -1, keepdims=True)
            if qt:
                peak = jnp.maximum(peak, jnp.max(s_f[rows], -1, keepdims=True))
            peak = peak * scale
            p_d = jnp.exp2(s_d * scale - peak)
            total = jnp.sum(p_d, -1, keepdims=True)
            if qt:
                p_f = jnp.exp2(s_f[rows] * scale - peak)
                total = total + jnp.sum(p_f, -1, keepdims=True)
                p_full.append(p_f.astype(BF))
            p_same.append(jnp.where(same, p_d, 0.0).astype(BF))
            p_earl.append(jnp.where(earlier, p_d, 0.0).astype(BF))
            recips.append(1.0 / total)
            logs = jnp.where(lane == h, peak + jnp.log2(total), logs)
        out = dot(jnp.concatenate(p_same, 0), vn[here, :])
        out = out + dot(jnp.concatenate(p_earl, 0), vc[here, :])
        if qt:
            out = out + dot(jnp.concatenate(p_full, 0), vc[: qt * TILE, :])
        out = out * jnp.concatenate(recips, 0)
        o[here, :] = unstack_heads(out, hm).astype(BF)
        lse[:, here] = logs.T[:8, :]


def attend(shift, q, kc, kn, vc, vn):
    length = q.shape[0]
    quads = q.shape[1] // QUAD
    col = pl.BlockSpec((length, QUAD), lambda g: (0, g))
    return pl.pallas_call(
        functools.partial(attend_kernel, length=length),
        grid=(quads,),
        in_specs=[pl.BlockSpec(memory_space=pltpu.SMEM)] + [col] * 5,
        out_specs=[col, pl.BlockSpec((8, length), lambda g: (g, 0))],
        out_shape=[
            jax.ShapeDtypeStruct((length, quads * QUAD), BF),
            jax.ShapeDtypeStruct((quads * 8, length), F32),
        ],
        compiler_params=params(),
        name="attend",
    )(shift, q, kc, kn, vc, vn)


GELU_C = 0.7978845608028654


def hidden_kernel(mix, tok, msk, vec, wo, wup, bias, n2, act, dg, rm, *, tile, chunk):
    masked = jnp.broadcast_to(msk[...], (tile, D)) > 0.5
    res = jnp.where(masked, vec[5:6, :], tok[...].astype(F32))
    res = res + dot(mix[...], wo[...])
    rm[...] = res
    x, _ = norm_rows(res)
    n = (x * (1.0 + vec[2:3, :]) + vec[3:4, :]).astype(BF)
    n2[...] = n
    for j in range(wup.shape[1] // chunk):
        cols = slice(j * chunk, (j + 1) * chunk)
        h = dot(n, wup[:, cols]) + bias[:, cols]
        h2 = h * h
        t = jnp.tanh(h * (GELU_C + (GELU_C * 0.044715) * h2))
        half = 0.5 + 0.5 * t
        act[:, cols] = (h * half).astype(BF)
        slope = half + (0.5 * h) * (1.0 - t * t) * (GELU_C + (3 * GELU_C * 0.044715) * h2)
        dg[:, cols] = slope.astype(BF)


def hidden(mixed, tokens, mask_col, vec, wo, wup, bias):
    length = tokens.shape[0]
    ff = wup.shape[1]
    tile = TILE
    rows = pl.BlockSpec((tile, D), lambda i: (i, 0))
    broad = pl.BlockSpec((tile, ff), lambda i: (i, 0))
    return pl.pallas_call(
        functools.partial(hidden_kernel, tile=tile, chunk=512),
        grid=(length // tile,),
        in_specs=[
            rows,
            rows,
            pl.BlockSpec((tile, 1), lambda i: (i, 0)),
            whole(vec.shape),
            whole(wo.shape),
            whole(wup.shape),
            whole(bias.shape),
        ],
        out_specs=[rows, broad, broad, rows],
        out_shape=[
            jax.ShapeDtypeStruct((length, D), BF),
            jax.ShapeDtypeStruct((length, ff), BF),
            jax.ShapeDtypeStruct((length, ff), BF),
            jax.ShapeDtypeStruct((length, D), F32),
        ],
        compiler_params=params(),
        name="hidden",
    )(mixed, tokens, mask_col, vec, wo, wup, bias)


def back_kernel(
    cot, wdn, wup, wo, dg, rm, vec, mix, gp, gmid, gb, gmix, delta, sums, bsum, *, tile, chunk
):
    first = pl.program_id(0) == 0

    @pl.when(first)
    def _():
        sums[...] = jnp.zeros_like(sums)
        bsum[...] = jnp.zeros_like(bsum)

    c = cot[...]
    grad_n = None
    for j in range(wup.shape[1] // chunk):
        cols = slice(j * chunk, (j + 1) * chunk)
        g = dot_t(c, wdn[cols, :]) * dg[:, cols].astype(F32)
        g = g.astype(BF)
        gp[:, cols] = g
        bsum[:, cols] += jnp.sum(g.astype(F32), 0, keepdims=True)
        part = dot_t(g, wup[:, cols])
        grad_n = part if grad_n is None else grad_n + part
    x, scale = norm_rows(rm[...])
    y = grad_n * (1.0 + vec[2:3, :])
    back = scale * (
        y - jnp.mean(y, -1, keepdims=True) - x * jnp.mean(y * x, -1, keepdims=True)
    )
    cf = c.astype(F32)
    mid = cf + back
    gmid[...] = mid
    low = mid.astype(BF)
    gb[...] = low
    sums[0:1, :] += jnp.sum(grad_n * x, 0, keepdims=True)
    sums[1:2, :] += jnp.sum(grad_n, 0, keepdims=True)
    sums[2:3, :] += jnp.sum(cf, 0, keepdims=True)
    gm = dot_t(low, wo[...]).astype(BF)
    gmix[...] = gm
    prod = gm.astype(F32) * mix[...].astype(F32)
    high = prod.astype(BF)
    rest = (prod - high.astype(F32)).astype(BF)
    row = lax.broadcasted_iota(jnp.int32, (32, D), 0)
    lane = lax.broadcasted_iota(jnp.int32, (32, D), 1)
    pick = jnp.where((row // 8 == lane // QUAD) & (row % 8 == (lane % QUAD) // HEAD_DIM), 1.0, 0.0)
    pick = pick.astype(BF)
    delta[...] = (dot_t(pick, high) + dot_t(pick, rest))[: delta.shape[0]]


def back(cot, wdn, wup, wo, dg, rm, vec, mixed):
    length = cot.shape[0]
    ff = wup.shape[1]
    tile = TILE
    rows = pl.BlockSpec((tile, D), lambda i: (i, 0))
    broad = pl.BlockSpec((tile, ff), lambda i: (i, 0))
    return pl.pallas_call(
        functools.partial(back_kernel, tile=tile, chunk=512),
        grid=(length // tile,),
        in_specs=[
            rows,
            whole(wdn.shape),
            whole(wup.shape),
            whole(wo.shape),
            broad,
            rows,
            whole(vec.shape),
            rows,
        ],
        out_specs=[
            broad,
            rows,
            rows,
            rows,
            pl.BlockSpec((24, tile), lambda i: (0, i)),
            whole((8, D)),
            whole((1, ff)),
        ],
        out_shape=[
            jax.ShapeDtypeStruct((length, ff), BF),
            jax.ShapeDtypeStruct((length, D), F32),
            jax.ShapeDtypeStruct((length, D), BF),
            jax.ShapeDtypeStruct((length, D), BF),
            jax.ShapeDtypeStruct((24, length), F32),
            jax.ShapeDtypeStruct((8, D), F32),
            jax.ShapeDtypeStruct((1, ff), F32),
        ],
        compiler_params=params(),
        name="back",
    )(cot, wdn, wup, wo, dg, rm, vec, mixed)


def outer_kernel(a, b, o):
    o[...] = t_dot(a[...], b[...]).astype(BF)


def outer_rows(a, b, block):
    length, width = a.shape
    n = b.shape[1]
    return pl.pallas_call(
        outer_kernel,
        grid=(width // block,),
        in_specs=[pl.BlockSpec((length, block), lambda i: (0, i)), whole(b.shape)],
        out_specs=pl.BlockSpec((block, n), lambda i: (i, 0)),
        out_shape=jax.ShapeDtypeStruct((width, n), BF),
        compiler_params=params(),
        name="outer_rows",
    )(a, b)


def outer_cols(a, b, block):
    length, width = a.shape
    n = b.shape[1]
    return pl.pallas_call(
        outer_kernel,
        grid=(n // block,),
        in_specs=[whole(a.shape), pl.BlockSpec((length, block), lambda i: (0, i))],
        out_specs=pl.BlockSpec((width, block), lambda i: (0, i)),
        out_shape=jax.ShapeDtypeStruct((width, n), BF),
        compiler_params=params(),
        name="outer_cols",
    )(a, b)


def attend_back_kernel(
    shift, q, kc, kn, vc, vn, do, lse, delta, cos, sin, msk, n1, nmt,
    gq, gk, gv, gm, gin, dkc, dvc, dkn, dvn, *, length
):
    hm = head_rows()
    sh = shift[0]
    kb = lax.broadcasted_iota(jnp.int32, (TILE, TILE), 0) >> sh
    qb = lax.broadcasted_iota(jnp.int32, (TILE, TILE), 1) >> sh
    same1, earl1 = kb == qb, kb < qb
    scale = SCORE_SCALE * LOG2E
    n_tiles = length // TILE
    keep_q = []
    for qt in range(n_tiles):
        here = slice(qt * TILE, (qt + 1) * TILE)
        qs = stack_heads(q[here, :], hm)
        ds_ = stack_heads(do[here, :], hm)
        lrow = jnp.concatenate([lse[h : h + 1, here] for h in range(4)], 1)
        drow = jnp.concatenate([delta[h : h + 1, here] for h in range(4)], 1)
        dq = None
        for kt in range(qt):
            there = slice(kt * TILE, (kt + 1) * TILE)
            p = jnp.exp2(dot_t(kc[there, :], qs) * scale - lrow)
            g = (p * (dot_t(vc[there, :], ds_) - drow)).astype(BF)
            dvc[there, :] += dot(p.astype(BF), ds_)
            dkc[there, :] += dot(g, qs)
            part = t_dot(g, kc[there, :])
            dq = part if dq is None else dq + part
        s_c, s_n = dot_t(kc[here, :], qs), dot_t(kn[here, :], qs)
        g_c, g_n = dot_t(vc[here, :], ds_), dot_t(vn[here, :], ds_)
        ps, pe, gs, ge = [], [], [], []
        for h in range(4):
            cols = slice(h * TILE, (h + 1) * TILE)
            s_d = jnp.where(same1, s_n[:, cols], s_c[:, cols])
            p = jnp.exp2(s_d * scale - lrow[:, cols])
            g = p * (jnp.where(same1, g_n[:, cols], g_c[:, cols]) - drow[:, cols])
            ps.append(jnp.where(same1, p, 0.0).astype(BF))
            pe.append(jnp.where(earl1, p, 0.0).astype(BF))
            gs.append(jnp.where(same1, g, 0.0).astype(BF))
            ge.append(jnp.where(earl1, g, 0.0).astype(BF))
        ps, pe, gs, ge = [jnp.concatenate(m, 1) for m in (ps, pe, gs, ge)]
        dvn[here, :] = dot(ps, ds_)
        dvc[here, :] = dot(pe, ds_)
        dkn[here, :] = dot(gs, qs)
        dkc[here, :] = dot(ge, qs)
        part = t_dot(gs, kn[here, :]) + t_dot(ge, kc[here, :])
        dq = part if dq is None else dq + part
        keep_q.append(unstack_heads(dq, hm))
    sums = [jnp.zeros((1, 128), F32) for _ in range(6)]
    for t in range(n_tiles):
        here = slice(t * TILE, (t + 1) * TILE)
        m = jnp.broadcast_to(msk[here, :], (TILE, 128))
        keep = 1.0 - m
        c, s = cos[here, :] * SCORE_SCALE, sin[here, :] * (-SCORE_SCALE)
        for i in range(2):
            lanes = slice(i * 128, (i + 1) * 128)
            r = turn(keep_q[t][:, lanes], c, s)
            gq[here, lanes] = (r * keep).astype(BF)
            sums[i] += jnp.sum(r * m, 0, keepdims=True)
            noisy = dkn[here, lanes]
            gk[here, lanes] = turn(dkc[here, lanes] + keep * noisy, c, s).astype(BF)
            sums[2 + i] += jnp.sum(turn(noisy * m, c, s), 0, keepdims=True)
            noisy = dvn[here, lanes]
            gv[here, lanes] = (dvc[here, lanes] + keep * noisy).astype(BF)
            sums[4 + i] += jnp.sum(noisy * m, 0, keepdims=True)
    total = jnp.concatenate(sums, 1)
    gm[...] = jnp.broadcast_to(total, gm.shape)
    column = nmt[...]
    for i, ref in enumerate((gq, gk, gv)):
        part = t_dot(n1[...], ref[...])
        for j in range(2):
            row = total[:, (2 * i + j) * 128 : (2 * i + j + 1) * 128]
            gin[i, :, j * 128 : (j + 1) * 128] = (
                part[:, j * 128 : (j + 1) * 128] + column * row
            ).astype(BF)


def attend_back(shift, q, kc, kn, vc, vn, do, lse, delta, cos, sin, mask_col, n1, nmt):
    length = q.shape[0]
    quads = q.shape[1] // QUAD
    col = pl.BlockSpec((length, QUAD), lambda g: (0, g))
    stat = pl.BlockSpec((8, length), lambda g: (g, 0))
    return pl.pallas_call(
        functools.partial(attend_back_kernel, length=length),
        grid=(quads,),
        in_specs=[pl.BlockSpec(memory_space=pltpu.SMEM)]
        + [col] * 6
        + [stat] * 2
        + [whole(cos.shape), whole(sin.shape), whole(mask_col.shape), whole(n1.shape), whole(nmt.shape)],
        out_specs=[col] * 3
        + [
            pl.BlockSpec((8, 3 * QUAD), lambda g: (g, 0)),
            pl.BlockSpec((3, D, QUAD), lambda g: (0, 0, g)),
        ],
        out_shape=[jax.ShapeDtypeStruct((length, D), BF)] * 3
        + [
            jax.ShapeDtypeStruct((quads * 8, 3 * QUAD), F32),
            jax.ShapeDtypeStruct((3, D, quads * QUAD), BF),
        ],
        scratch_shapes=[pltpu.VMEM((length, QUAD), F32)] * 4,
        compiler_params=params(),
        name="attend_back",
    )(shift, q, kc, kn, vc, vn, do, lse, delta, cos, sin, mask_col, n1, nmt)


def final_kernel(gq, gk, gv, gm, w, tok, msk, vec, gmid, tgrad, sums, *, tile):
    i = pl.program_id(0)
    gain = 1.0 + vec[0:1, :]

    @pl.when(i == 0)
    def _():
        total = None
        for g in range(3):
            for part in range(3):
                row = gm[8 * g : 8 * g + 8, part * QUAD : (part + 1) * QUAD]
                high = row.astype(BF)
                rest = (row - high.astype(F32)).astype(BF)
                cols = slice(part * D + g * QUAD, part * D + (g + 1) * QUAD)
                both = jnp.concatenate([high, rest], 0)
                add = dot_t(both, w[:, cols])
                total = add if total is None else total + add
        y = total[0:1] + total[8:9]
        x, scale = norm_rows(vec[5:6, :])
        qv = y * gain
        row = scale * (
            qv - jnp.mean(qv, -1, keepdims=True) - x * jnp.mean(qv * x, -1, keepdims=True)
        )
        sums[...] = jnp.concatenate([y * x, y, row, jnp.zeros((5, D), F32)], 0)

    y = dot_t(gq[...], w[:, :D]) + dot_t(gk[...], w[:, D : 2 * D]) + dot_t(gv[...], w[:, 2 * D :])
    x, scale = norm_rows(tok[...].astype(F32))
    qv = y * gain
    row = scale * (
        qv - jnp.mean(qv, -1, keepdims=True) - x * jnp.mean(qv * x, -1, keepdims=True)
    )
    m = jnp.broadcast_to(msk[...], (tile, D))
    mid = gmid[...]
    tgrad[...] = row + (1.0 - m) * mid
    sums[0:1, :] += jnp.sum(y * x, 0, keepdims=True)
    sums[1:2, :] += jnp.sum(y, 0, keepdims=True)
    sums[2:3, :] += jnp.sum(m * mid, 0, keepdims=True)


def final(gq, gk, gv, gm, w, tokens, mask_col, vec, gmid):
    length = tokens.shape[0]
    tile = TILE
    rows = pl.BlockSpec((tile, D), lambda i: (i, 0))
    return pl.pallas_call(
        functools.partial(final_kernel, tile=tile),
        grid=(length // tile,),
        in_specs=[
            rows, rows, rows, whole(gm.shape), whole(w.shape), rows,
            pl.BlockSpec((tile, 1), lambda i: (i, 0)), whole(vec.shape), rows,
        ],
        out_specs=[rows, whole((8, D))],
        out_shape=[
            jax.ShapeDtypeStruct((length, D), F32),
            jax.ShapeDtypeStruct((8, D), F32),
        ],
        compiler_params=params(),
        name="final",
    )(gq, gk, gv, gm, w, tokens, mask_col, vec, gmid)


MESH = pl.DeviceIdType.MESH
PLAN = ((0, 2), (1, 1), (2, 2), (3, 2))


def flip(index, bit):
    return index + bit - 2 * bit * lax.rem(lax.div(index, bit), 2)


def remote(src, dst, send, recv, device):
    return pltpu.make_async_remote_copy(
        src_ref=src, dst_ref=dst, send_sem=send, recv_sem=recv, device_id=device, device_id_type=MESH
    )


def attend_tile(qt, lanes, stat, masks, hm, q, kc, kn, vc, vn, o, lse):
    same, earlier = masks
    scale = SCORE_SCALE * LOG2E
    lane = lax.broadcasted_iota(jnp.int32, (TILE, 128), 1)
    here, past = slice(qt * TILE, (qt + 1) * TILE), slice(0, qt * TILE)
    qs = stack_heads(q[here, lanes], hm)
    s_c = dot_t(qs, kc[here, lanes])
    s_n = dot_t(qs, kn[here, lanes])
    if qt:
        s_f = dot_t(qs, kc[past, lanes])
    p_full, p_same, p_earl, recips = [], [], [], []
    logs = jnp.zeros((TILE, 128), F32)
    for h in range(4):
        rows = slice(h * TILE, (h + 1) * TILE)
        s_d = jnp.where(same, s_n[rows], jnp.where(earlier, s_c[rows], NEG_FILL))
        peak = jnp.max(s_d, -1, keepdims=True)
        if qt:
            peak = jnp.maximum(peak, jnp.max(s_f[rows], -1, keepdims=True))
        peak = peak * scale
        p_d = jnp.exp2(s_d * scale - peak)
        total = jnp.sum(p_d, -1, keepdims=True)
        if qt:
            p_f = jnp.exp2(s_f[rows] * scale - peak)
            total = total + jnp.sum(p_f, -1, keepdims=True)
            p_full.append(p_f.astype(BF))
        p_same.append(jnp.where(same, p_d, 0.0).astype(BF))
        p_earl.append(jnp.where(earlier, p_d, 0.0).astype(BF))
        recips.append(1.0 / total)
        logs = jnp.where(lane == h, peak + jnp.log2(total), logs)
    out = dot(jnp.concatenate(p_same, 0), vn[here, lanes])
    out = out + dot(jnp.concatenate(p_earl, 0), vc[here, lanes])
    if qt:
        out = out + dot(jnp.concatenate(p_full, 0), vc[past, lanes])
    out = out * jnp.concatenate(recips, 0)
    o[here, lanes] = unstack_heads(out, hm).astype(BF)
    lse[stat, here] = logs.T[:8, :]


def gather_kernel(
    block_shift, tok, msk, cos, sin, small, own_in, own_out, own_up, own_dn,
    n1_o, q_o, kc_o, kn_o, vc_o, vn_o, mixed, lse, nmt, vec, w_in, w_out, w_up, w_dn,
    n1, q, kc, kn, vc, vn, held, w, smalls, f_in, f_out, f_up, f_dn, b_out, b_up, b_dn,
    own_send, own_recv, send, recv, small_send, small_recv, local, done,
    *, tile,
):
    wide, me = lax.axis_index("wide"), lax.axis_index("narrow")
    xp, cp, yp = (wide, flip(me, 2)), (wide, flip(me, 1)), (flip(wide, 1), me)
    dp = (wide, flip(flip(me, 2), 1))
    mine = lax.rem(wide, 2)
    parts, fulls = (own_in, own_out, own_up, own_dn), (w, w_out, w_up, w_dn)
    wides = (f_in, f_out, f_up, f_dn)
    loads = [pltpu.make_async_copy(parts[i], wides[i], local.at[i]) for i in range(4)]
    for copy in loads:
        copy.start()

    barrier = pltpu.get_barrier_semaphore()
    for peer in (xp, cp, yp, dp):
        pl.semaphore_signal(barrier, inc=1, device_id=peer, device_id_type=MESH)
    pl.semaphore_wait(barrier, 4)

    tiny = [
        remote(small, smalls.at[k], small_send.at[k], small_recv.at[k], peer)
        for k, peer in enumerate((cp, xp, dp))
    ]
    for copy in tiny:
        copy.start()

    rows_in = own_in.shape[0]
    spot_in = pl.ds(pl.multiple_of(me * rows_in, rows_in), rows_in)
    loads[0].wait()
    w[spot_in, :] = f_in[...].astype(BF)
    owns = (w.at[spot_in], b_out, b_up, b_dn)

    def rows_of(matrix, owner, half, chunk, chunks):
        rows = parts[matrix].shape[0]
        step = rows // (2 * chunks)
        return pl.ds(pl.multiple_of(owner * rows + half * (rows // 2) + chunk * step, step), step)

    chunks = []
    for matrix, count in PLAN:
        for chunk in range(count):
            at = len(chunks)
            full = fulls[matrix]
            if matrix:
                src = owns[matrix].at[rows_of(matrix, 0, mine, chunk, count)]
            else:
                src = w.at[rows_of(matrix, me, mine, chunk, count)]
            here = rows_of(matrix, me, mine, chunk, count)
            got = rows_of(matrix, flip(me, 2), mine, chunk, count)
            other = rows_of(matrix, flip(me, 2), 1 - mine, chunk, count)
            chunks.append(
                (
                    remote(src, full.at[here], send.at[at, 0], recv.at[at, 0], xp),
                    remote(full.at[got], full.at[got], send.at[at, 1], recv.at[at, 1], yp),
                    remote(full.at[got], full.at[got], send.at[at, 2], recv.at[at, 2], cp),
                    remote(full.at[other], full.at[other], send.at[at, 3], recv.at[at, 3], cp),
                )
            )
    whole_own, kept = [], []
    for matrix in range(4):
        rows = parts[matrix].shape[0]
        spot = pl.ds(pl.multiple_of(me * rows, rows), rows)
        whole_own.append(
            remote(owns[matrix], fulls[matrix].at[spot], own_send.at[matrix], own_recv.at[matrix], cp)
        )
        if matrix:
            kept.append(pltpu.make_async_copy(owns[matrix], fulls[matrix].at[spot], local.at[3 + matrix]))

    chunks[0][0].start()
    chunks[1][0].start()
    whole_own[0].start()

    def advance(i):
        chunks[i][0].wait_recv()
        chunks[i][1].start()
        chunks[i][2].start()
        if i + 2 < len(chunks):
            chunks[i + 2][0].start()

    def hand_on(i):
        chunks[i][1].wait_recv()
        chunks[i][3].start()

    for matrix, low in ((1, b_out), (2, b_up), (3, b_dn)):
        loads[matrix].wait()
        low[...] = wides[matrix][...].astype(BF)
    advance(0)
    for copy in tiny:
        copy.wait_recv()
    total = small[...].astype(F32)
    for k in range(3):
        total = total + smalls[k].astype(F32)
    vec[...] = total
    gain, shift = 1.0 + vec[0:1, :], vec[1:2, :]
    x_m, _ = norm_rows(vec[5:6, :])
    n_m = (x_m * gain + shift).astype(BF)
    wide_row = jnp.broadcast_to(n_m.astype(F32), (128, D))
    nmt[...] = wide_row.T
    advance(1)
    hand_on(0)
    length = tok.shape[0]
    for t in range(length // tile):
        here = slice(t * tile, (t + 1) * tile)
        x, _ = norm_rows(tok[here, :].astype(F32))
        n1[here, :] = (x * gain + shift).astype(BF)
    outs = []

    def put(src, dst):
        copy = pltpu.make_async_copy(src, dst, done.at[len(outs)])
        copy.start()
        outs.append(copy)

    put(n1, n1_o)
    hand_on(1)
    whole_own[0].wait_recv()
    for i in range(2):
        chunks[i][2].wait_recv()
        chunks[i][3].wait_recv()
    put(w, w_in)
    for matrix in (1, 2, 3):
        whole_own[matrix].start()
        kept[matrix - 1].start()

    held[...] = dot(wide_row[:16].astype(BF), w[...])

    def columns(t):
        here = slice(t * tile, (t + 1) * tile)
        n = n1[here, :]
        masked = jnp.broadcast_to(msk[here, :], (tile, 128)) > 0.5
        c, s = cos[here, :], sin[here, :]
        for j in range(3 * D // 256):
            p = dot(n, w[:, j * 256 : (j + 1) * 256])
            for i in range(2):
                col = j * 256 + i * 128
                lanes = slice(col % D, col % D + 128)
                clean = p[:, i * 128 : (i + 1) * 128]
                row = jnp.broadcast_to(held[0:1, col : col + 128], (tile, 128))
                if col < D:
                    q[here, lanes] = jnp.where(masked, turn(row, c, s), turn(clean, c, s)).astype(BF)
                elif col < 2 * D:
                    clean = turn(clean, c, s)
                    kc[here, lanes] = clean.astype(BF)
                    kn[here, lanes] = jnp.where(masked, turn(row, c, s), clean).astype(BF)
                else:
                    vc[here, lanes] = clean.astype(BF)
                    vn[here, lanes] = jnp.where(masked, row, clean).astype(BF)

    steps = length // tile
    for t in range(steps):
        columns(t)
        if t == 2:
            advance(2)
    for src, dst in ((q, q_o), (kc, kc_o), (kn, kn_o), (vc, vc_o), (vn, vn_o)):
        put(src, dst)
    hm = head_rows()
    sh = block_shift[0]
    rb = lax.broadcasted_iota(jnp.int32, (TILE, TILE), 0) >> sh
    cb = lax.broadcasted_iota(jnp.int32, (TILE, TILE), 1) >> sh
    masks = (rb == cb, cb < rb)
    last = len(chunks)
    tasks = []
    for i in range(3, last):
        tasks.append((advance, i))
        tasks.append((hand_on, i - 1))
    tasks.append((hand_on, last - 1))
    for g in range(D // QUAD):
        for qt in range(steps):
            lanes = slice(g * QUAD, (g + 1) * QUAD)
            stat = slice(8 * g, 8 * g + 8)
            attend_tile(qt, lanes, stat, masks, hm, q, kc, kn, vc, vn, mixed, lse)
            if tasks:
                step, i = tasks.pop(0)
                step(i)
    for step, i in tasks:
        step(i)
    for matrix in (1, 2, 3):
        whole_own[matrix].wait_recv()
        kept[matrix - 1].wait()
    for i in range(2, len(chunks)):
        chunks[i][2].wait_recv()
        chunks[i][3].wait_recv()
    for chunk in chunks:
        for copy in chunk:
            copy.wait_send()
    for copy in whole_own + tiny:
        copy.wait_send()
    for copy in outs:
        copy.wait()


def gather_attend(block_shift, tokens, mask_col, cos, sin, small, owns, narrow):
    length = tokens.shape[0]
    vm = pl.BlockSpec(memory_space=pltpu.VMEM)
    hb = pl.BlockSpec(memory_space=pl.ANY)
    n_chunks = sum(count for _, count in PLAN)
    rows = jax.ShapeDtypeStruct((length, D), BF)
    fulls = [jax.ShapeDtypeStruct((o.shape[0] * narrow, o.shape[1]), BF) for o in owns]
    return pl.pallas_call(
        functools.partial(gather_kernel, tile=TILE),
        in_specs=[pl.BlockSpec(memory_space=pltpu.SMEM)] + [vm] * 5 + [hb] * 4,
        out_specs=[hb] * 6 + [vm] * 4 + [hb] * 4,
        out_shape=[rows] * 7
        + [
            jax.ShapeDtypeStruct((D // QUAD * 8, length), F32),
            jax.ShapeDtypeStruct((D, 128), F32),
            jax.ShapeDtypeStruct((16, D), F32),
        ]
        + fulls,
        scratch_shapes=[pltpu.VMEM((length, D), BF)] * 6
        + [
            pltpu.VMEM((16, 3 * D), F32),
            pltpu.VMEM((D, 3 * D), BF),
            pltpu.VMEM((3, 16, D), BF),
        ]
        + [pltpu.VMEM(o.shape, F32) for o in owns]
        + [pltpu.VMEM(o.shape, BF) for o in owns[1:]]
        + [
            pltpu.SemaphoreType.DMA((4,)),
            pltpu.SemaphoreType.DMA((4,)),
            pltpu.SemaphoreType.DMA((n_chunks, 4)),
            pltpu.SemaphoreType.DMA((n_chunks, 4)),
            pltpu.SemaphoreType.DMA((3,)),
            pltpu.SemaphoreType.DMA((3,)),
            pltpu.SemaphoreType.DMA((7,)),
            pltpu.SemaphoreType.DMA((7,)),
        ],
        compiler_params=pltpu.CompilerParams(
            collective_id=0, has_side_effects=True, vmem_limit_bytes=VMEM_LIMIT
        ),
        name="gather_attend",
    )(block_shift, tokens, mask_col, cos, sin, small, *owns)


def rotary_tables(length):
    half = HEAD_DIM // 2
    inverse = 10000.0 ** (-2.0 * np.arange(half, dtype=np.float64) / HEAD_DIM)
    angles = np.arange(length, dtype=np.float64)[:, None] * inverse[None, :]
    cos, sin = np.cos(angles), np.sin(angles)
    cos = np.concatenate([cos, cos], 1)
    sin = np.concatenate([-sin, sin], 1)
    return (
        np.concatenate([cos, cos], 1).astype(np.float32),
        np.concatenate([sin, sin], 1).astype(np.float32),
    )


def adam_update(master, moment, square, gradient, factor, rate, decay):
    clipped = gradient * factor
    first_new = BETA_ONE * moment + (1.0 - BETA_ONE) * clipped
    second_new = BETA_TWO * square + (1.0 - BETA_TWO) * clipped * clipped
    first_hat = first_new / (1.0 - BETA_ONE**ADAM_STEP)
    second_hat = second_new / (1.0 - BETA_TWO**ADAM_STEP)
    master_new = master - rate * (first_hat / (jnp.sqrt(second_hat) + ADAM_EPS) + decay * master)
    return (first_new, second_new, master_new)


def shards(
    tokens, noise_mask, block_shift, cotangent,
    input_weight, input_moment, input_square,
    output_weight, output_moment, output_square,
    up_weight, up_moment, up_square,
    down_weight, down_moment, down_square,
    up_bias, bias_moment, bias_square,
    vectors, vector_moment, vector_square,
):
    length = tokens.shape[0]
    narrow = lax.axis_size("narrow")
    spot = lax.axis_index("narrow")
    small = jnp.zeros((16, D), BF)
    small = lax.dynamic_update_slice(small, vectors.astype(BF), (0, spot * vectors.shape[1]))
    small = lax.dynamic_update_slice(small, up_bias.astype(BF)[None, :], (8 + spot, 0))
    cos, sin = [jnp.asarray(t) for t in rotary_tables(length)]
    mask_col = noise_mask.astype(F32)[:, None]
    owns = (input_weight, output_weight, up_weight, down_weight)
    n1, q, kc, kn, vc, vn, mixed, lse, nmt, vec, w_in, w_out, w_up, w_dn = gather_attend(
        block_shift, tokens, mask_col, cos, sin, small, owns, narrow
    )
    bias = vec[8:12].reshape(1, -1)
    vec = vec[:8]
    n2, act, dg, rm = hidden(mixed, tokens, mask_col, vec, w_out, w_up, bias)
    g_down = outer_rows(act, cotangent, 512)
    gp, gmid, gb, gmix, delta, sums2, bsum = back(
        cotangent, w_dn, w_up, w_out, dg, rm, vec, mixed
    )
    g_up = outer_cols(n2, gp, 512)
    g_out = outer_cols(mixed, gb, 768)
    gq, gk, gv, gm, gin = attend_back(
        block_shift, q, kc, kn, vc, vn, gmix, lse, delta, cos, sin, mask_col, n1, nmt
    )
    token_grad, sums1 = final(gq, gk, gv, gm, w_in, tokens, mask_col, vec, gmid)
    g_in = jnp.concatenate([gin[0], gin[1], gin[2]], 1)
    vector_grad = jnp.stack(
        [sums1[0], sums1[1], sums2[0], sums2[1], sums2[2], sums1[2]], 0
    )
    shares = [
        lax.psum_scatter(g, "narrow", scatter_dimension=0, tiled=True)
        for g in (g_in, g_out, g_up, g_down)
    ]
    reduced = [lax.psum(s, "wide").astype(F32) for s in shares]
    small = jnp.concatenate([bsum.reshape(-1, D), vector_grad], 0)
    small = lax.psum(small, ("wide", "narrow"))
    rows = bsum.shape[1] // D
    per = up_bias.shape[0]
    bias_share = lax.dynamic_slice_in_dim(small[:rows].reshape(-1), spot * per, per)
    vector_share = lax.dynamic_slice_in_dim(small[rows:], spot * vectors.shape[1], vectors.shape[1], 1)
    square_sum = jnp.sum(vector_share * vector_share) + jnp.sum(bias_share * bias_share)
    for member in reduced:
        square_sum = square_sum + jnp.sum(member * member)
    grad_norm = jnp.sqrt(lax.psum(square_sum, "narrow"))
    factor = jnp.minimum(1.0, CLIP_LIMIT / (grad_norm + 1e-06))
    out = [grad_norm.reshape(1), token_grad]
    for w, m, s, g, rate, decay in (
        (input_weight, input_moment, input_square, reduced[0], MATRIX_RATE, MATRIX_DECAY),
        (output_weight, output_moment, output_square, reduced[1], MATRIX_RATE, MATRIX_DECAY),
        (up_weight, up_moment, up_square, reduced[2], MATRIX_RATE, MATRIX_DECAY),
        (down_weight, down_moment, down_square, reduced[3], MATRIX_RATE, MATRIX_DECAY),
        (up_bias, bias_moment, bias_square, bias_share, VECTOR_RATE, 0.0),
        (vectors, vector_moment, vector_square, vector_share, VECTOR_RATE, 0.0),
    ):
        out.extend(adam_update(w, m, s, g, factor, rate, decay))
    return tuple(out)


def solution(mesh):
    both = ("wide", "narrow")
    rows = P("narrow", None)
    in_specs = (
        (P(both, None), P(both), P(both), P(both, None))
        + (rows,) * 12
        + (P("narrow"),) * 3
        + (P(None, "narrow"),) * 3
    )
    out_specs = (P(), P(both, None)) + (rows,) * 12 + (P("narrow"),) * 3 + (P(None, "narrow"),) * 3
    return jax.shard_map(shards, mesh=mesh, in_specs=in_specs, out_specs=out_specs, check_vma=False)
```

profile of v0, /device:TPU:0, one launch (start us, length us, event | category | flops | bytes accessed | tf_op | source)
XLA Modules:
  0.0 519.0 jit_solution(15295625021701925072)
XLA Ops:
  7.2 0.7 convert_element_type.22
  9.3 1.0 copy.44.msk
  12.2 70.0 %gather_attend.1 = (bf16[1024,768]{1,0:T(8,128)(2,1)}, bf16[1024,768]{1,0:T(8,128)(2,1)}, bf16[1024,768]{1,0:T(8,128)(2,1)}, bf16[1024,768]{1,0:T(8,128)(2,1)}, ...) custom-call(s32[1]{0:T(128)S(6)} %copy.55.block_shift.shift, ...), custom_call_target="tpu_custom_call" | custom-call | tf_op jit(solution)/shard_map/gather_attend/pallas_call | solution.py:797
  82.2 1.3 slice.35.vec
  83.6 0.7 slice_bitcast_fusion.3
  84.9 19.5 %hidden.1 = (bf16[1024,768]{1,0:T(8,128)(2,1)}, bf16[1024,3072]{1,0:T(8,128)(2,1)}, bf16[1024,3072]{1,0:T(8,128)(2,1)}, f32[1024,768]{1,0:T(8,128)}) custom-call(bf16[1024,768]{1,0:T(8,128)(2,1)} %get-tuple-element.55.mix.a, bf16[1024,768]{1,0:T(8,128)(2,1)} %tok.5, f32[1024,1]{1,0:T(8,128)} %copy.44.msk, f32[8,768]{1,0:T(8,128)} %slice.35.vec, ...), custom_call_target="tpu_custom_call" | custom-call | tf_op jit(solution)/shard_map/hidden/pallas_call | solution.py:240
  104.5 23.5 %back.1 = (bf16[1024,3072]{1,0:T(8,128)(2,1)}, f32[1024,768]{1,0:T(8,128)}, bf16[1024,768]{1,0:T(8,128)(2,1)}, bf16[1024,768]{1,0:T(8,128)(2,1)}, f32[24,1024]{1...) custom-call(bf16[1024,768]{1,0:T(8,128)(2,1)} %b.1, bf16[3072,768]{1,0:T(8,128)(2,1)} %get-tuple-element.52.wdn, ...), custom_call_target="tpu_custom_call" | custom-call | tf_op jit(solution)/shard_map/back/pallas_call | solution.py:315
  128.0 4.3 outer_cols.2
  132.4 46.1 %attend_back.1 = (bf16[1024,768]{1,0:T(8,128)(2,1)}, bf16[1024,768]{1,0:T(8,128)(2,1)}, bf16[1024,768]{1,0:T(8,128)(2,1)}, f32[24,768]{1,0:T(8,128)}, bf16[3,768,768]{2,1,0:T(8,128)(2,1)}) custom-call(s32[1]{0:T(128)S(6)} %copy.55.block_shift.shift, bf16[1024,768]{1,0:T(8,128)(2,1)} %get-tuple-element.60.q, bf16[1024,768]{1,0:T(8,128)(2,1)} %get-tuple-element.61.kc, ...), custom_call_target="tpu_custom_call" | custom-call | tf_op jit(solution)/shard_map/attend_back/pallas_call | solution.py:464
  178.5 2.2 slice_bitcast_fusion.2
  180.7 1.9 pad_maximum_fusion
  182.7 9.9 %outer_cols.3 = bf16[768,3072]{1,0:T(8,128)(2,1)} custom-call(bf16[1024,768]{1,0:T(8,128)(2,1)} %get-tuple-element.80.a, bf16[1024,3072]{1,0:T(8,128)(2,1)} %get-tuple-element.81.b), custom_call_target="tpu_custom_call" | custom-call | tf_op jit(solution)/shard_map/outer_cols/pallas_call | solution.py:372
  192.7 10.6 %outer_rows.1 = bf16[3072,768]{1,0:T(8,128)(2,1)} custom-call(bf16[1024,3072]{1,0:T(8,128)(2,1)} %get-tuple-element.82.a, bf16[1024,768]{1,0:T(8,128)(2,1)} %b.1), custom_call_target="tpu_custom_call" | custom-call | tf_op jit(solution)/shard_map/outer_rows/pallas_call | solution.py:358
  203.4 22.4 %reduce-scatter.5.cloned.1.call-done = bf16[192,2304]{1,0:T(8,128)(2,1)} async-done(((bf16[768,2304]{1,0:T(8,128)(2,1)}), bf16[192,2304]{1,0:T(8,128)(2,1)}) %reduce-scatter.5.cloned.1.call-update) | async-done | bytes 884752 | tf_op jit(solution)/shard_map/reduce_scatter | solution.py:895
  225.8 50.4 %reduce-scatter.9.cloned.1.call-done = bf16[192,3072]{1,0:T(8,128)(2,1)} async-done(((bf16[768,3072]{1,0:T(8,128)(2,1)}), bf16[192,3072]{1,0:T(8,128)(2,1)}) %reduce-scatter.9.cloned.1.call-update) | async-done | bytes 1179664 | tf_op jit(solution)/shard_map/reduce_scatter | solution.py:895
  276.2 50.4 %reduce-scatter.11.cloned.1.call-done = bf16[768,768]{1,0:T(8,128)(2,1)} async-done(((bf16[3072,768]{1,0:T(8,128)(2,1)}), bf16[768,768]{1,0:T(8,128)(2,1)}) %reduce-scatter.11.cloned.1.call-update) | async-done | bytes 1179664 | tf_op jit(solution)/shard_map/reduce_scatter | solution.py:895
  326.7 11.4 %final.1 = (f32[1024,768]{1,0:T(8,128)}, f32[8,768]{1,0:T(8,128)}) custom-call(bf16[1024,768]{1,0:T(8,128)(2,1)} %get-tuple-element.70.gq, bf16[1024,768]{1,0:T(8,128)(2,1)} %get-tuple-element.71.gk, bf16[1024,768]{1,0:T(8,128)(2,1)} %get-tuple-element.72.gv, f32[24,768]{1,0:T(8,128)} %get-tuple-element.73.gm, bf16[768,2304]{1,0:T(8,128)(2,1)} %get-tuple-element.74.w, ...), custom_call_target="tpu_custom_call" | custom-call | tf_op jit(solution)/shard_map/final/pallas_call | solution.py:529
  338.1 0.9 slice.37
  339.0 0.7 slice.39
  341.0 44.3 %psum.42 = f32[10,768]{1,0:T(8,128)S(1)} all-reduce(f32[10,768]{1,0:T(8,128)S(1)} %pad_maximum_fusion.1), channel_id=1, replica_groups=mesh['wide'=8,'narrow'=4] {'wide','narrow'}, use_global_device_ids=true, to_apply=%region_0.0 | all-reduce | flops 7680 | bytes 61440 | tf_op jit(solution)/shard_map/psum | solution.py:900
  388.0 83.8 %all-reduce.3.cloned.1.call-done = (bf16[192,2304]{1,0:T(8,128)(2,1)}, bf16[192,768]{1,0:T(8,128)(2,1)}, bf16[192,3072]{1,0:T(8,128)(2,1)}, bf16[768,768]{1,0:T(8,128)(2,1)}) async-done(((bf16[192,2304]{1,0:T(8,128)(2,1)}, bf16[192,768]{1,0:T(8,128)(2,1)}, bf16[192,3072]{1,0:T(8,128)(2,1)}, bf16[768,768]{1,0:T(8,128)(2,1)}), (bf16[192,2304]{1,0:T(8,128)(2,1)}, bf16[192,768]{1,0:T(8,128)(2,1)}, ...) | async-done | bytes 3538960 | tf_op jit(solution)/shard_map/psum | solution.py:898
  471.9 2.3 fusion.10
  474.2 1.7 fusion.14
  475.9 2.5 fusion.4
  478.4 2.5 fusion.5
  483.5 7.4 %psum.47 = f32[]{:T(128)} all-reduce(f32[]{:T(128)S(6)} %add.147), channel_id=1, replica_groups=mesh['wide'=8,'narrow'=4] {'narrow'}, use_global_device_ids=true, to_apply=%region_15.0 | all-reduce | flops 1 | bytes 8 | tf_op jit(solution)/shard_map/psum | solution.py:908
  491.6 1.5 multiply_subtract_fusion.4
  493.0 1.4 multiply_subtract_fusion.5
  494.5 6.7 %multiply_subtract_fusion = (f32[768,768]{1,0:T(8,128)}, f32[768,768]{1,0:T(8,128)}, f32[768,768]{1,0:T(8,128)}) fusion(f32[768,768]{1,0:T(8,128)S(1)} %copy-done, f32[]{:T(128)S(6)} %min.3, bf16[768,768]{1,0:T(8,128)(2,1)S(1)} %copy-done.4, f32[768,768]{1,0:T(8,128)} %param.39, f32[768,768]{1,0:T(8,128)} %param.38), kind=kLoop, calls=%fused_computation.16 | loop fusion | flops 10027008 | bytes 15335428 | tf_op jit(solution)/shard_map/sub | solution.py:852
  501.2 4.2 multiply_subtract_fusion.1
  505.5 1.5 multiply_subtract_fusion.3
  507.9 3.3 multiply_subtract_fusion.2
  (66 shorter events, 7.0 us)
Async XLA Ops:
  7.2 196.2 %reduce-scatter.7.cloned.1.call-start = ((), (), s32[]{:S(2)}) async-start(), calls=%async_computation.5 | async-start | bytes 1474560 | tf_op jit(solution)/shard_map/reduce_scatter | solution.py:895
  11.6 0.6 copy-start.14
  132.4 93.4 %reduce-scatter.5.cloned.1.call-start = ((), (), s32[]{:S(2)}) async-start(), calls=%async_computation.4 | async-start | bytes 4423680 | tf_op jit(solution)/shard_map/reduce_scatter | solution.py:895
  182.6 93.6 %reduce-scatter.9.cloned.1.call-start = ((), (), s32[]{:S(2)}) async-start(), calls=%async_computation.6 | async-start | bytes 5898240 | tf_op jit(solution)/shard_map/reduce_scatter | solution.py:895
  192.7 134.0 %reduce-scatter.11.cloned.1.call-start = ((), (), s32[]{:S(2)}) async-start(), calls=%async_computation.7 | async-start | bytes 5898240 | tf_op jit(solution)/shard_map/reduce_scatter | solution.py:895
  203.3 268.5 %all-reduce.3.cloned.1.call-start = ((), (), s32[]{:S(2)}) async-start(), calls=%async_computation.8 | async-start | bytes 7077888 | tf_op jit(solution)/shard_map/psum | solution.py:898
  326.7 13.6 %copy-start.17 = (f32[1,3072]{1,0:T(1,128)S(1)}, f32[1,3072]{1,0:T(1,128)}, u32[]{:S(2)}) copy-start(f32[1,3072]{1,0:T(1,128)} %get-tuple-element.59) | copy-start | bytes 36868
  326.7 14.3 %copy-start.18 = (f32[8,768]{1,0:T(8,128)S(1)}, f32[8,768]{1,0:T(8,128)}, u32[]{:S(2)}) copy-start(f32[8,768]{1,0:T(8,128)} %get-tuple-element.77) | copy-start | bytes 73732
  338.1 154.9 %copy-start.16 = (f32[768]{0:T(1024)S(1)}, f32[768]{0:T(1024)}, u32[]{:S(2)}) copy-start(f32[768]{0:T(1024)} %param.40) | copy-start | bytes 9220
  338.1 156.3 %copy-start = (f32[768,768]{1,0:T(8,128)S(1)}, f32[768,768]{1,0:T(8,128)}, u32[]{:S(2)}) copy-start(f32[768,768]{1,0:T(8,128)} %own_dn.1) | copy-start | bytes 7077892
  385.3 2.7 copy-start.15
  471.9 22.6 %copy-start.4 = (bf16[768,768]{1,0:T(8,128)(2,1)S(1)}, bf16[768,768]{1,0:T(8,128)(2,1)}, u32[]{:S(2)}) copy-start(bf16[768,768]{1,0:T(8,128)(2,1)} %get-tuple-element.87) | copy-start | bytes 3538948
  494.4 6.7 %copy-start.1 = (f32[192,3072]{1,0:T(8,128)S(1)}, f32[192,3072]{1,0:T(8,128)}, u32[]{:S(2)}) copy-start(f32[192,3072]{1,0:T(8,128)} %own_up.1) | copy-start | bytes 7077892
  494.4 6.7 %copy-start.3 = (bf16[192,3072]{1,0:T(8,128)(2,1)S(1)}, bf16[192,3072]{1,0:T(8,128)(2,1)}, u32[]{:S(2)}) copy-start(bf16[192,3072]{1,0:T(8,128)(2,1)} %get-tuple-element.86) | copy-start | bytes 3538948
  494.4 6.7 %copy-start.7 = (f32[192,3072]{1,0:T(8,128)S(1)}, f32[192,3072]{1,0:T(8,128)}, u32[]{:S(2)}) copy-start(f32[192,3072]{1,0:T(8,128)} %param.36) | copy-start | bytes 7077892
  494.4 6.7 %copy-start.8 = (f32[192,3072]{1,0:T(8,128)S(1)}, f32[192,3072]{1,0:T(8,128)}, u32[]{:S(2)}) copy-start(f32[192,3072]{1,0:T(8,128)} %param.35) | copy-start | bytes 7077892
  501.2 4.3 copy-start.6
  501.2 4.3 copy-start.11
  501.2 4.3 copy-start.12
  501.2 4.3 copy-start.13
  501.2 5.8 %copy-start.9 = (f32[192,2304]{1,0:T(8,128)S(1)}, f32[192,2304]{1,0:T(8,128)}, u32[]{:S(2)}) copy-start(f32[192,2304]{1,0:T(8,128)} %param.30) | copy-start | bytes 5308420
  501.2 5.8 %copy-start.10 = (f32[192,2304]{1,0:T(8,128)S(1)}, f32[192,2304]{1,0:T(8,128)}, u32[]{:S(2)}) copy-start(f32[192,2304]{1,0:T(8,128)} %param.29) | copy-start | bytes 5308420
  505.5 2.2 copy-start.2
  505.5 2.4 copy-start.5
Sparse Core Ops, SparseCore 0:
  132.5 28.2 reduce-scatter.6
  182.7 42.9 reduce-scatter.4
  228.3 47.8 reduce-scatter.8
  278.8 47.8 reduce-scatter.10
  330.4 141.3 all-reduce.2
where the time goes:
time: 526 us; the launch traced here: 519 us
  waiting for transfers between devices  207 us (39%)
  Pallas kernels  195 us (37%)
  blocking collectives  51.7 us (10%)
  other arithmetic  33.6 us (6%)
  between operations  20.7 us (4%)
  local copies, waits for them, and re-layouts  10.2 us (2%)
    reduce_scatter x4, waiting for transfers between devices, shards(): lax.psum_scatter(g, 'narrow', scatter_dimension=0, tiled=True)  123 us
    psum x1, waiting for transfers between devices, shards(): reduced = [lax.psum(s, 'wide').astype(F32) for s in shares]  83.8 us
    pallas_call x1, Pallas kernels, gather_attend(): pl.pallas_call(functools.partial(gather_kernel, tile=TILE), in_specs=[pl....  70 us
    pallas_call x1, Pallas kernels, attend_back(): pl.pallas_call(functools.partial(attend_back_kernel, length=length), grid...  46.1 us
    psum x1, blocking collectives, shards(): small = lax.psum(small, ('wide', 'narrow'))  44.3 us
    pallas_call x1, Pallas kernels, back(): pl.pallas_call(functools.partial(back_kernel, tile=tile, chunk=512), grid...  23.5 us
    pallas_call x1, Pallas kernels, hidden(): pl.pallas_call(functools.partial(hidden_kernel, tile=tile, chunk=512), gr...  19.5 us
    sub x6, other arithmetic, adam_update(): master - rate * (first_hat / (jnp.sqrt(second_hat) + ADAM_EPS) + decay *...  18.5 us
  transfers between devices with their start and end apart: 5, of which 4 were waited for; matrix products, arithmetic and copies ran while one was open for 2% of the time, Pallas kernels for 15%

commit v1 on v0

--- a/solution.py
+++ b/solution.py
@@ -830,6 +830,526 @@
     )(block_shift, tokens, mask_col, cos, sin, small, *owns)
 
 
+class Chunk:
+    def __init__(self, index, rows, base, slot, env):
+        self.rows, self.base, self.slot, self.env = rows, base, slot, env
+        e = env
+        half, quart, wid = rows // 2, rows // 4, D // 2
+        rs = pl.ds(0, rows)
+        self.mine_half = pl.ds(pl.multiple_of(e.y * half, half), half)
+        other_half = pl.ds(pl.multiple_of((1 - e.y) * half, half), half)
+
+        def quad(z, top):
+            return (
+                pl.ds(pl.multiple_of(top + e.y * half + lax.div(z, 2) * quart, quart), quart),
+                pl.ds(pl.multiple_of(lax.rem(z, 2) * wid, wid), wid),
+            )
+
+        self.quad = quad(e.z, 0)
+        sem = lambda k: (e.send.at[index, k], e.recv.at[index, k])
+        self.core = remote(slot.at[1 - e.c, :, rs], e.got_c[index], *sem(0), e.cp)
+        self.over_x = remote(slot.at[e.c, 1 - e.x, rs], e.got_x[index], *sem(1), e.xp)
+        self.over_y = remote(
+            slot.at[e.c, e.x, other_half], e.got_y[index], *sem(2), e.yp
+        )
+        self.over_z, self.back_z = [], []
+        place = quad(e.z, base)
+        self.place = place
+        for k in range(3):
+            r, l = quad(e.zs[k], 0)
+            self.over_z.append(
+                remote(
+                    slot.at[e.c, e.x, r, l], e.got_z[index].at[k], *sem(3 + k), e.zp[k]
+                )
+            )
+            self.back_z.append(
+                remote(e.out.at[place], e.out.at[place], *sem(6 + k), e.zp[k])
+            )
+        rows_y = pl.ds(pl.multiple_of(base + e.y * half, half), half)
+        self.back_y = remote(e.out.at[rows_y], e.out.at[rows_y], *sem(9), e.yp)
+        self.index = index
+
+    def start(self):
+        self.core.start()
+
+    def core_in(self):
+        e, rs = self.env, pl.ds(0, self.rows)
+        self.core.wait_recv()
+        for j in range(2):
+            there = (e.c, j, rs)
+            self.slot[there] = (
+                self.slot[there].astype(F32) + e.got_c[self.index][j].astype(F32)
+            ).astype(BF)
+        self.over_x.start()
+
+    def x_in(self):
+        e, rs = self.env, pl.ds(0, self.rows)
+        self.over_x.wait_recv()
+        there = (e.c, e.x, rs)
+        self.slot[there] = (
+            self.slot[there].astype(F32) + e.got_x[self.index][...].astype(F32)
+        ).astype(BF)
+        self.over_y.start()
+
+    def y_in(self):
+        e = self.env
+        self.over_y.wait_recv()
+        there = (e.c, e.x, self.mine_half)
+        self.slot[there] = (
+            self.slot[there].astype(F32) + e.got_y[self.index][...].astype(F32)
+        ).astype(BF)
+        for copy in self.over_z:
+            copy.start()
+
+    def z_in(self):
+        e = self.env
+        for copy in self.over_z:
+            copy.wait_recv()
+        total = self.slot[(e.c, e.x) + self.quad].astype(F32)
+        for k in range(3):
+            total = total + e.got_z[self.index][k].astype(F32)
+        e.out[self.place] = total.astype(BF)
+        for copy in self.back_z:
+            copy.start()
+        self.core.wait_send()
+        self.over_x.wait_send()
+        self.over_y.wait_send()
+        for copy in self.over_z:
+            copy.wait_send()
+
+    def z_back(self):
+        for copy in self.back_z:
+            copy.wait_recv()
+        self.back_y.start()
+
+    def y_back(self):
+        e = self.env
+        self.back_y.wait_recv()
+        part = e.out[self.base : self.base + self.rows, :].astype(F32)
+        part = part * part
+        total = e.square[...]
+        for i in range(self.rows // 8):
+            for j in range(D // 128):
+                total = total + part[i * 8 : i * 8 + 8, j * 128 : j * 128 + 128]
+        e.square[...] = total
+
+    def finish(self):
+        for copy in self.back_z + [self.back_y]:
+            copy.wait_send()
+
+
+class Env:
+    pass
+
+
+CHUNKS = (
+    [(256, 256 * j) for j in range(3)]
+    + [(192, 768 + 192 * j) for j in range(4)]
+    + [(192, 1536)]
+    + [(192, 1728 + 192 * j) for j in range(3)]
+)
+SLOTS = 4
+GRAD_ROWS = 2304
+
+
+def grad_scores_tile(qt, lanes, stat, masks, hm, q, kc, kn, vc, vn, do, lse, delta, dkc, dvc, dkn, dvn):
+    same1, earl1 = masks
+    scale = SCORE_SCALE * LOG2E
+    here = slice(qt * TILE, (qt + 1) * TILE)
+    qs = stack_heads(q[here, lanes], hm)
+    ds_ = stack_heads(do[here, lanes], hm)
+    lrow = jnp.concatenate([lse[stat + h : stat + h + 1, here] for h in range(4)], 1)
+    drow = jnp.concatenate([delta[stat + h : stat + h + 1, here] for h in range(4)], 1)
+    dq = None
+    for kt in range(qt):
+        there = slice(kt * TILE, (kt + 1) * TILE)
+        p = jnp.exp2(dot_t(kc[there, lanes], qs) * scale - lrow)
+        g = (p * (dot_t(vc[there, lanes], ds_) - drow)).astype(BF)
+        dvc[there, :] += dot(p.astype(BF), ds_)
+        dkc[there, :] += dot(g, qs)
+        part = t_dot(g, kc[there, lanes])
+        dq = part if dq is None else dq + part
+    s_c, s_n = dot_t(kc[here, lanes], qs), dot_t(kn[here, lanes], qs)
+    g_c, g_n = dot_t(vc[here, lanes], ds_), dot_t(vn[here, lanes], ds_)
+    ps, pe, gs, ge = [], [], [], []
+    for h in range(4):
+        cols = slice(h * TILE, (h + 1) * TILE)
+        s_d = jnp.where(same1, s_n[:, cols], s_c[:, cols])
+        p = jnp.exp2(s_d * scale - lrow[:, cols])
+        g = p * (jnp.where(same1, g_n[:, cols], g_c[:, cols]) - drow[:, cols])
+        ps.append(jnp.where(same1, p, 0.0).astype(BF))
+        pe.append(jnp.where(earl1, p, 0.0).astype(BF))
+        gs.append(jnp.where(same1, g, 0.0).astype(BF))
+        ge.append(jnp.where(earl1, g, 0.0).astype(BF))
+    ps, pe, gs, ge = [jnp.concatenate(m, 1) for m in (ps, pe, gs, ge)]
+    dvn[here, :] = dot(ps, ds_)
+    dvc[here, :] = dot(pe, ds_)
+    dkn[here, :] = dot(gs, qs)
+    dkc[here, :] = dot(ge, qs)
+    part = t_dot(gs, kn[here, lanes]) + t_dot(ge, kc[here, lanes])
+    dq = part if dq is None else dq + part
+    return unstack_heads(dq, hm)
+
+
+def layer_norm_back(y, gain, x, scale):
+    t = y * gain
+    return scale * (t - jnp.mean(t, -1, keepdims=True) - x * jnp.mean(t * x, -1, keepdims=True))
+
+
+def reduce_kernel(
+    block_shift, lse, delta, cos, sin, msk, vec, nmt, sums2, bsum,
+    q_h, kc_h, kn_h, vc_h, vn_h, do_h, n1_h, w_h, tok_h, gmid_h, gdn_h, gup_h, gout_h,
+    out, tgrad_h, norm, small,
+    q, kc, kn, vc, vn, do, n1, w, tok, grads, gms, dkc, dvc, dkn, dvn, keep_q,
+    slots, own_slots, big_c, big_x, big_y, big_z, few_c, few_x, few_y, few_z, got_s, square, got_n, mine_n,
+    send, recv, small_send, small_recv, load, slot_load, done,
+    *, length, alone,
+):
+    e = Env()
+    wide, me = lax.axis_index("wide"), lax.axis_index("narrow")
+    e.x, e.c, e.y = lax.div(me, 2), lax.rem(me, 2), lax.rem(wide, 2)
+    e.z = lax.rem(lax.div(wide, 2), 4)
+    e.xp, e.cp, e.yp = (wide, flip(me, 2)), (wide, flip(me, 1)), (flip(wide, 1), me)
+    dp = (wide, flip(flip(me, 2), 1))
+    e.zp = [(flip(wide, 2), me), (flip(wide, 4), me), (flip(flip(wide, 2), 4), me)]
+    e.zs = [flip(e.z, 1), flip(e.z, 2), flip(flip(e.z, 1), 2)]
+    e.send, e.recv, e.out, e.square = send, recv, out, square
+    e.got_c, e.got_x, e.got_y, e.got_z = [
+        [(big.at[i] if i < 3 else few.at[i - 3]) for i in range(len(CHUNKS))]
+        for big, few in ((big_c, few_c), (big_x, few_x), (big_y, few_y), (big_z, few_z))
+    ]
+
+    loads = {}
+
+    def fetch(name, src, dst):
+        copy = pltpu.make_async_copy(src, dst, load.at[len(loads)])
+        copy.start()
+        loads[name] = copy
+
+    n_chunks = len(CHUNKS)
+    ready = n_chunks - 3
+    first = []
+    for i, (rows, base) in enumerate(CHUNKS):
+        slot = slots.at[i % SLOTS] if i < ready else own_slots.at[i - ready]
+        first.append(Chunk(i, rows, base, slot, e))
+    slot_loads = {}
+
+    def fill(i):
+        rows = CHUNKS[i][0]
+        copies = []
+        for c in range(2):
+            for x in range(2):
+                n = 2 * x + c
+                if i < 3:
+                    src = gdn_h.at[768 * n + 256 * i : 768 * n + 256 * i + 256]
+                elif i < 7:
+                    src = gup_h.at[192 * n : 192 * n + 192, 768 * (i - 3) : 768 * (i - 2)]
+                else:
+                    src = gout_h.at[192 * n : 192 * n + 192]
+                copies.append(
+                    pltpu.make_async_copy(
+                        src, slots.at[i % SLOTS, c, x, 0:rows], slot_load.at[i % SLOTS, 2 * c + x]
+                    )
+                )
+        for copy in copies:
+            copy.start()
+        slot_loads[i] = copies
+
+    def filled(i):
+        for copy in slot_loads[i]:
+            copy.wait()
+        first[i].start()
+
+    for i in range(2):
+        fill(i)
+
+    def fetch_quad(g):
+        lanes = slice(g * QUAD, (g + 1) * QUAD)
+        for k, (src, dst) in enumerate(
+            ((q_h, q), (kc_h, kc), (kn_h, kn), (vc_h, vc), (vn_h, vn), (do_h, do))
+        ):
+            fetch((g, k), src.at[:, lanes], dst.at[:, lanes])
+
+    fetch_quad(0)
+    for i in range(2, SLOTS):
+        fill(i)
+
+    barrier = pltpu.get_barrier_semaphore()
+    peers = [e.xp, e.cp, e.yp, dp] + e.zp
+    for peer in peers:
+        pl.semaphore_signal(barrier, inc=1, device_id=peer, device_id_type=MESH)
+    pl.semaphore_wait(barrier, len(peers))
+
+    square[...] = jnp.zeros_like(square)
+    filled(0)
+    filled(1)
+    fetch_quad(1)
+    fetch_quad(2)
+    fetch("n1", n1_h, n1)
+    first[0].core_in()
+    first[1].core_in()
+    filled(2)
+    filled(3)
+
+    queue = []
+    for h in range(2 * n_chunks + 6):
+        b = h // 2
+        if h % 2 == 0:
+            queue.append(
+                [("x_in", b), ("core_in", b + 2), ("z_in", b - 1), ("fill", b + 3), ("y_back", b - 2)]
+            )
+        else:
+            queue.append([("y_in", b), ("filled", b + 3), ("z_back", b - 1)])
+    state = {"h": 0, "made": ready}
+
+    def beat():
+        if state["h"] >= len(queue):
+            return
+        for action, i in queue[state["h"]]:
+            if i < 0 or i >= n_chunks:
+                continue
+            if action == "fill":
+                if SLOTS <= i < ready:
+                    fill(i)
+            elif action == "filled":
+                if 4 <= i < ready:
+                    filled(i)
+            else:
+                getattr(first[i], action)()
+        state["h"] += 1
+
+    hm = head_rows()
+    sh = block_shift[0]
+    kb = lax.broadcasted_iota(jnp.int32, (TILE, TILE), 0) >> sh
+    qb = lax.broadcasted_iota(jnp.int32, (TILE, TILE), 1) >> sh
+    masks = (kb == qb, kb < qb)
+    n_tiles = length // TILE
+
+    def finish_quad(g):
+        sums = [jnp.zeros((1, 128), F32) for _ in range(6)]
+        for t in range(n_tiles):
+            here = slice(t * TILE, (t + 1) * TILE)
+            m = jnp.broadcast_to(msk[here, :], (TILE, 128))
+            keep = 1.0 - m
+            c, s = cos[here, :] * SCORE_SCALE, sin[here, :] * (-SCORE_SCALE)
+            for i in range(2):
+                lanes = slice(i * 128, (i + 1) * 128)
+                to = slice(g * QUAD + i * 128, g * QUAD + (i + 1) * 128)
+                r = turn(keep_q[here, lanes], c, s)
+                grads[0, here, to] = (r * keep).astype(BF)
+                sums[i] += jnp.sum(r * m, 0, keepdims=True)
+                noisy = dkn[here, lanes]
+                grads[1, here, to] = turn(dkc[here, lanes] + keep * noisy, c, s).astype(BF)
+                sums[2 + i] += jnp.sum(turn(noisy * m, c, s), 0, keepdims=True)
+                noisy = dvn[here, lanes]
+                grads[2, here, to] = (dvc[here, lanes] + keep * noisy).astype(BF)
+                sums[4 + i] += jnp.sum(noisy * m, 0, keepdims=True)
+        total = jnp.concatenate(sums, 1)
+        gms[8 * g : 8 * g + 8, :] = jnp.broadcast_to(total, (8, 3 * QUAD))
+        column = nmt[...]
+        at = ready + g
+        slot = own_slots.at[g]
+        for i in range(3):
+            part = t_dot(n1[...], grads[i, :, g * QUAD : (g + 1) * QUAD])
+            for j in range(2):
+                row = total[:, (2 * i + j) * 128 : (2 * i + j + 1) * 128]
+                full = (part[:, j * 128 : (j + 1) * 128] + column * row).astype(BF)
+                for n in range(4):
+                    slot[n % 2, n // 2, 0:192, i * 256 + j * 128 : i * 256 + (j + 1) * 128] = full[
+                        192 * n : 192 * (n + 1)
+                    ]
+        first[at].start()
+
+    for g in range(D // QUAD):
+        for k in range(6):
+            loads[(g, k)].wait()
+        lanes = slice(g * QUAD, (g + 1) * QUAD)
+        for qt in range(n_tiles):
+            keep_q[qt * TILE : (qt + 1) * TILE, :] = grad_scores_tile(
+                qt, lanes, 8 * g, masks, hm, q, kc, kn, vc, vn, do, lse, delta, dkc, dvc, dkn, dvn
+            )
+            beat()
+            if qt == 3:
+                beat()
+        if g == 0:
+            loads["n1"].wait()
+            fetch("w", w_h, w)
+            fetch("tok", tok_h, tok)
+        finish_quad(g)
+    for k, f in enumerate((dkc, dvc, dkn)):
+        fetch(("mid", k), gmid_h.at[:, k * QUAD : (k + 1) * QUAD], f)
+
+    gain = 1.0 + vec[0:1, :]
+    loads["w"].wait()
+    loads["tok"].wait()
+    for k in range(3):
+        loads[("mid", k)].wait()
+    total = None
+    for g in range(3):
+        for part in range(3):
+            row = gms[8 * g : 8 * g + 8, part * QUAD : (part + 1) * QUAD]
+            high = row.astype(BF)
+            rest = (row - high.astype(F32)).astype(BF)
+            cols = slice(part * D + g * QUAD, part * D + (g + 1) * QUAD)
+            add = dot_t(jnp.concatenate([high, rest], 0), w[:, cols])
+            total = add if total is None else total + add
+    y = total[0:1] + total[8:9]
+    x, scale = norm_rows(vec[5:6, :])
+    g1, s1, mrow = y * x, y, layer_norm_back(y, gain, x, scale)
+    outs = []
+    for t in range(n_tiles):
+        here = slice(t * TILE, (t + 1) * TILE)
+        y = None
+        for part in range(3):
+            add = dot_t(grads[part, here, :], w[:, part * D : (part + 1) * D])
+            y = add if y is None else y + add
+        x, scale = norm_rows(tok[here, :].astype(F32))
+        row = layer_norm_back(y, gain, x, scale)
+        g1 = g1 + jnp.sum(y * x, 0, keepdims=True)
+        s1 = s1 + jnp.sum(y, 0, keepdims=True)
+        adds = []
+        for k, f in enumerate((dkc, dvc, dkn)):
+            m = jnp.broadcast_to(msk[here, :], (TILE, QUAD))
+            mid = f[here, :]
+            adds.append(jnp.sum(m * mid, 0, keepdims=True))
+            f[here, :] = row[:, k * QUAD : (k + 1) * QUAD] + (1.0 - m) * mid
+            copy = pltpu.make_async_copy(
+                f.at[here, :], tgrad_h.at[here, k * QUAD : (k + 1) * QUAD], done.at[t, k]
+            )
+            copy.start()
+            outs.append(copy)
+        mrow = mrow + jnp.concatenate(adds, 1)
+        beat()
+    rows = [g1, s1, sums2[0:1, :], sums2[1:2, :], sums2[2:3, :], mrow, jnp.zeros((2, D), F32)]
+    rows += [bsum[:, j * D : (j + 1) * D] for j in range(4)] + [jnp.zeros((4, D), F32)]
+    small[...] = jnp.concatenate(rows, 0)
+    hops = []
+    for group in ([e.cp], [e.xp], [e.yp], e.zp):
+        hop = []
+        for peer in group:
+            k = sum(len(m) for m in hops) + len(hop)
+            hop.append(remote(got_s.at[0, len(hops)], got_s.at[1, k], small_send.at[k], small_recv.at[k], peer))
+        hops.append(hop)
+    for k, hop in enumerate(hops):
+        got_s[0, k] = small[...]
+        for copy in hop:
+            copy.start()
+        if state["h"] < len(queue):
+            beat()
+        for copy in hop:
+            copy.wait_recv()
+        total = small[...]
+        for j in range(len(hop)):
+            total = total + got_s[1, sum(len(m) for m in hops[:k]) + j]
+        small[...] = total
+    while state["h"] < len(queue):
+        beat()
+    lane = lax.broadcasted_iota(jnp.int32, (16, D), 1)
+    row = lax.broadcasted_iota(jnp.int32, (16, D), 0)
+    own = ((row < 6) & (lane >= me * 192) & (lane < me * 192 + 192)) | (row == 8 + me)
+    part = jnp.where(own, small[...], 0.0)
+    whole_sum = jnp.sum(square[...]) + jnp.sum(part * part)
+    mine_n[...] = jnp.full((8, 128), whole_sum, F32)
+    last = [
+        remote(mine_n, got_n.at[k], small_send.at[6 + k], small_recv.at[6 + k], peer)
+        for k, peer in enumerate((e.cp, e.xp, dp))
+    ]
+    for copy in last:
+        copy.start()
+    for copy in last:
+        copy.wait_recv()
+    norm[...] = jnp.sqrt(mine_n[...] + got_n[0] + got_n[1] + got_n[2])
+    for chunk in first:
+        chunk.finish()
+    for hop in hops:
+        for copy in hop:
+            copy.wait_send()
+    for copy in last:
+        copy.wait_send()
+    for copy in outs:
+        copy.wait()
+
+
+def attend_reduce(
+    block_shift, lse, delta, cos, sin, mask_col, vec, nmt, sums2, bsum,
+    q, kc, kn, vc, vn, do, n1, w_in, tokens, gmid, g_down, g_up, g_out,
+):
+    length = q.shape[0]
+    vm = pl.BlockSpec(memory_space=pltpu.VMEM)
+    hb = pl.BlockSpec(memory_space=pl.ANY)
+    n = len(CHUNKS)
+    return pl.pallas_call(
+        functools.partial(reduce_kernel, length=length, alone=True),
+        in_specs=[pl.BlockSpec(memory_space=pltpu.SMEM)] + [vm] * 9 + [hb] * 13,
+        out_specs=[vm, hb, vm, vm],
+        out_shape=[
+            jax.ShapeDtypeStruct((GRAD_ROWS, D), BF),
+            jax.ShapeDtypeStruct((length, D), F32),
+            jax.ShapeDtypeStruct((8, 128), F32),
+            jax.ShapeDtypeStruct((16, D), F32),
+        ],
+        scratch_shapes=[pltpu.VMEM((length, D), BF)] * 7
+        + [
+            pltpu.VMEM((D, 3 * D), BF),
+            pltpu.VMEM((length, D), BF),
+            pltpu.VMEM((3, length, D), BF),
+            pltpu.VMEM((24, 3 * QUAD), F32),
+        ]
+        + [pltpu.VMEM((length, QUAD), F32)] * 5
+        + [
+            pltpu.VMEM((SLOTS, 2, 2, 256, D), BF),
+            pltpu.VMEM((3, 2, 2, 192, D), BF),
+        ]
+        + [
+            pltpu.VMEM((count,) + shape, BF)
+            for count, rows in ((3, 256), (n - 3, 192))
+            for shape in ((2, rows, D), (rows, D), (rows // 2, D), (3, rows // 4, D // 2))
+        ]
+        + [
+            pltpu.VMEM((2, 6, 16, D), F32),
+            pltpu.VMEM((8, 128), F32),
+            pltpu.VMEM((3, 8, 128), F32),
+            pltpu.VMEM((8, 128), F32),
+            pltpu.SemaphoreType.DMA((n, 10)),
+            pltpu.SemaphoreType.DMA((n, 10)),
+            pltpu.SemaphoreType.DMA((9,)),
+            pltpu.SemaphoreType.DMA((9,)),
+            pltpu.SemaphoreType.DMA((24,)),
+            pltpu.SemaphoreType.DMA((SLOTS, 4)),
+            pltpu.SemaphoreType.DMA((length // TILE, 3)),
+        ],
+        compiler_params=pltpu.CompilerParams(
+            collective_id=1, has_side_effects=True, vmem_limit_bytes=60 * 1024 * 1024
+        ),
+        name="attend_reduce",
+    )(
+        block_shift, lse, delta, cos, sin, mask_col, vec, nmt, sums2, bsum,
+        q, kc, kn, vc, vn, do, n1, w_in, tokens, gmid, g_down, g_up, g_out,
+    )
+
+
+def adam_kernel(norm, w, m, s, g, w_o, m_o, s_o, *, rate, decay):
+    factor = jnp.minimum(1.0, CLIP_LIMIT / (norm[0] + 1e-06))
+    first, second, master = adam_update(
+        w[...], m[...], s[...], g[...].astype(F32), factor, rate, decay
+    )
+    m_o[...], s_o[...], w_o[...] = first, second, master
+
+
+def adam(norm, w, m, s, grads, grid, w_block, w_map, g_block, g_map):
+    spec = pl.BlockSpec(w_block, w_map)
+    master, first, second = pl.pallas_call(
+        functools.partial(adam_kernel, rate=MATRIX_RATE, decay=MATRIX_DECAY),
+        grid=grid,
+        in_specs=[pl.BlockSpec(memory_space=pltpu.SMEM)] + [spec] * 3 + [pl.BlockSpec(g_block, g_map)],
+        out_specs=[spec] * 3,
+        out_shape=[jax.ShapeDtypeStruct(w.shape, F32)] * 3,
+        compiler_params=params(len(grid)),
+        name="adam",
+    )(norm, w, m, s, grads)
+    return first, second, master
+
+
 def rotary_tables(length):
     half = HEAD_DIM // 2
     inverse = 10000.0 ** (-2.0 * np.arange(half, dtype=np.float64) / HEAD_DIM)
@@ -883,40 +1403,46 @@
     )
     g_up = outer_cols(n2, gp, 512)
     g_out = outer_cols(mixed, gb, 768)
-    gq, gk, gv, gm, gin = attend_back(
-        block_shift, q, kc, kn, vc, vn, gmix, lse, delta, cos, sin, mask_col, n1, nmt
-    )
-    token_grad, sums1 = final(gq, gk, gv, gm, w_in, tokens, mask_col, vec, gmid)
-    g_in = jnp.concatenate([gin[0], gin[1], gin[2]], 1)
-    vector_grad = jnp.stack(
-        [sums1[0], sums1[1], sums2[0], sums2[1], sums2[2], sums1[2]], 0
-    )
-    shares = [
-        lax.psum_scatter(g, "narrow", scatter_dimension=0, tiled=True)
-        for g in (g_in, g_out, g_up, g_down)
-    ]
-    reduced = [lax.psum(s, "wide").astype(F32) for s in shares]
-    small = jnp.concatenate([bsum.reshape(-1, D), vector_grad], 0)
-    small = lax.psum(small, ("wide", "narrow"))
-    rows = bsum.shape[1] // D
-    per = up_bias.shape[0]
-    bias_share = lax.dynamic_slice_in_dim(small[:rows].reshape(-1), spot * per, per)
-    vector_share = lax.dynamic_slice_in_dim(small[rows:], spot * vectors.shape[1], vectors.shape[1], 1)
-    square_sum = jnp.sum(vector_share * vector_share) + jnp.sum(bias_share * bias_share)
-    for member in reduced:
-        square_sum = square_sum + jnp.sum(member * member)
-    grad_norm = jnp.sqrt(lax.psum(square_sum, "narrow"))
-    factor = jnp.minimum(1.0, CLIP_LIMIT / (grad_norm + 1e-06))
-    out = [grad_norm.reshape(1), token_grad]
-    for w, m, s, g, rate, decay in (
-        (input_weight, input_moment, input_square, reduced[0], MATRIX_RATE, MATRIX_DECAY),
-        (output_weight, output_moment, output_square, reduced[1], MATRIX_RATE, MATRIX_DECAY),
-        (up_weight, up_moment, up_square, reduced[2], MATRIX_RATE, MATRIX_DECAY),
-        (down_weight, down_moment, down_square, reduced[3], MATRIX_RATE, MATRIX_DECAY),
-        (up_bias, bias_moment, bias_square, bias_share, VECTOR_RATE, 0.0),
-        (vectors, vector_moment, vector_square, vector_share, VECTOR_RATE, 0.0),
+    grads, token_grad, norm, small = attend_reduce(
+        block_shift, lse, delta, cos, sin, mask_col, vec, nmt, sums2, bsum,
+        q, kc, kn, vc, vn, gmix, n1, w_in, tokens, gmid, g_down, g_up, g_out,
+    )
+    wide = lax.axis_size("wide")
+    per, per_v = up_bias.shape[0], vectors.shape[1]
+    if wide > 8:
+        groups = [[i + 8 * j for j in range(wide // 8)] for i in range(8)]
+        grads = lax.psum(grads, "wide", axis_index_groups=groups)
+        small = lax.psum(small, "wide", axis_index_groups=groups)
+    bias_share = lax.dynamic_slice(small, (8 + spot, 0), (1, per))[0]
+    vector_share = lax.dynamic_slice(small, (0, spot * per_v), (6, per_v))
+    norm = norm[0, :1]
+    if wide > 8:
+        squares = jnp.sum(jnp.square(grads.astype(F32)))
+        squares = squares + jnp.sum(bias_share * bias_share) + jnp.sum(vector_share * vector_share)
+        norm = jnp.sqrt(lax.psum(squares, "narrow")).reshape(1)
+    factor = jnp.minimum(1.0, CLIP_LIMIT / (norm[0] + 1e-06))
+    out = [norm, token_grad]
+    out += adam(
+        norm, input_weight, input_moment, input_square, grads, (3, 3),
+        (192, QUAD), lambda g, p: (0, 3 * p + g), (192, QUAD), lambda g, p: (9 + g, p),
+    )
+    out += adam(
+        norm, output_weight, output_moment, output_square, grads, (1,),
+        (192, D), lambda i: (0, 0), (192, D), lambda i: (8, 0),
+    )
+    out += adam(
+        norm, up_weight, up_moment, up_square, grads, (4,),
+        (192, D), lambda j: (0, j), (192, D), lambda j: (4 + j, 0),
+    )
+    out += adam(
+        norm, down_weight, down_moment, down_square, grads, (3,),
+        (256, D), lambda i: (i, 0), (256, D), lambda i: (i, 0),
+    )
+    for w, m, s, g in (
+        (up_bias, bias_moment, bias_square, bias_share),
+        (vectors, vector_moment, vector_square, vector_share),
     ):
-        out.extend(adam_update(w, m, s, g, factor, rate, decay))
+        out.extend(adam_update(w, m, s, g, factor, VECTOR_RATE, 0.0))
     return tuple(out)
 
 

time: 526 us -> 338 us (0.64)
  waiting for transfers between devices: 207 us -> 0 us
  Pallas kernels: 195 us -> 318 us
  blocking collectives: 51.7 us -> 0 us
  other arithmetic: 33.6 us -> 4.88 us
  between operations: 20.7 us -> 2.34 us
    reduce_scatter x4 -> x0, waiting for transfers between devices: 123 us -> none  [shards(): lax.psum_scatter(g, 'narrow', scatter_dimension=0, tiled=True)]
    pallas_call x2 -> x5, Pallas kernels: 57.5 us -> 179 us  [the longest x1 148 us: attend_reduce(): pl.pallas_call(functools.partial(reduce_kernel, length=length, alone=True...]
    psum x1 -> x0, waiting for transfers between devices: 83.8 us -> none  [shards(): reduced = [lax.psum(s, 'wide').astype(F32) for s in shares]]
    psum x2 -> x0, blocking collectives: 51.7 us -> none  [the longest x1 44.3 us: shards(): small = lax.psum(small, ('wide', 'narrow'))]
    sub x6 -> x2, other arithmetic: 18.5 us -> 2.04 us  [adam_update(): master - rate * (first_hat / (jnp.sqrt(second_hat) + ADAM_EPS) + decay *...]
    reduce_sum x6 -> x0, other arithmetic: 10.4 us -> none  [the longest x4 9 us: shards(): square_sum = square_sum + jnp.sum(member * member)]
  transfers between devices with their start and end apart: 5 -> 0, of which waited for: 4 -> 0; matrix products, arithmetic and copies ran while one was open for 2% -> 0% of each run, Pallas kernels for 15% -> 0%
where the time goes in v1:
time: 338 us; the launch traced here: 332 us
  Pallas kernels  318 us (94%)
  local copies, waits for them, and re-layouts  7.07 us (2%)
  other arithmetic  4.88 us (1%)
    pallas_call x1, Pallas kernels, attend_reduce(): pl.pallas_call(functools.partial(reduce_kernel, length=length, alone=True...  148 us
    pallas_call x1, Pallas kernels, gather_attend(): pl.pallas_call(functools.partial(gather_kernel, tile=TILE), in_specs=[pl....  71 us
    pallas_call x4, Pallas kernels, adam(): pl.pallas_call(functools.partial(adam_kernel, rate=MATRIX_RATE, decay=MAT...  31.2 us
    pallas_call x1, Pallas kernels, back(): pl.pallas_call(functools.partial(back_kernel, tile=tile, chunk=512), grid...  23.5 us
    pallas_call x1, Pallas kernels, hidden(): pl.pallas_call(functools.partial(hidden_kernel, tile=tile, chunk=512), gr...  19.6 us
    pallas_call x2, Pallas kernels, outer_cols(): pl.pallas_call(outer_kernel, grid=(n // block,), in_specs=[whole(a.shape)...  14.6 us
    pallas_call x1, Pallas kernels, outer_rows(): pl.pallas_call(outer_kernel, grid=(width // block,), in_specs=[pl.BlockSp...  9.97 us

profile of v1, /device:TPU:0, one launch (start us, length us, event | category | flops | bytes accessed | tf_op | source)
XLA Modules:
  0.0 332.0 jit_solution(17329876406418316751)
XLA Ops:
  1.3 0.7 convert_element_type.11
  2.0 0.7 convert_element_type.9
  2.7 0.7 convert_element_type.10
  3.4 0.4 dynamic_update_slice.6
  3.8 0.1 dynamic_update_slice.7.small
  3.8 0.0 copy-start.1
  3.9 1.0 copy.44.msk
  4.9 71.0 %gather_attend.1 = (bf16[1024,768]{1,0:T(8,128)(2,1)}, bf16[1024,768]{1,0:T(8,128)(2,1)}, bf16[1024,768]{1,0:T(8,128)(2,1)}, bf16[1024,768]{1,0:T(8,128)(2,1)}, ...) custom-call(s32[1]{0:T(128)S(6)} %copy.51.block_shift, ...), custom_call_target="tpu_custom_call" | custom-call | tf_op jit(solution)/shard_map/gather_attend/pallas_call | solution.py:797
  75.9 0.7 slice_bitcast_fusion
  76.7 1.3 slice.9.vec
  78.0 0.6 copy.47
  78.6 19.6 %hidden.1 = (bf16[1024,768]{1,0:T(8,128)(2,1)}, bf16[1024,3072]{1,0:T(8,128)(2,1)}, bf16[1024,3072]{1,0:T(8,128)(2,1)}, f32[1024,768]{1,0:T(8,128)}) custom-call(bf16[1024,768]{1,0:T(8,128)(2,1)} %get-tuple-element.65.mix.a, bf16[1024,768]{1,0:T(8,128)(2,1)} %tok_h.1, f32[1024,1]{1,0:T(8,128)} %copy.44.msk, f32[8,768]{1,0:T(8,128)} %slice.9.vec, ...), custom_call_target="tpu_custom_call" | custom-call | tf_op jit(solution)/shard_map/hidden/pallas_call | solution.py:240
  98.2 23.5 %back.1 = (bf16[1024,3072]{1,0:T(8,128)(2,1)}, f32[1024,768]{1,0:T(8,128)}, bf16[1024,768]{1,0:T(8,128)(2,1)}, bf16[1024,768]{1,0:T(8,128)(2,1)}, f32[24,1024]{1...) custom-call(bf16[1024,768]{1,0:T(8,128)(2,1)} %b.1, bf16[3072,768]{1,0:T(8,128)(2,1)} %get-tuple-element.62.wdn, ...), custom_call_target="tpu_custom_call" | custom-call | tf_op jit(solution)/shard_map/back/pallas_call | solution.py:315
  121.7 10.0 %outer_rows.1.gdn_h = bf16[3072,768]{1,0:T(8,128)(2,1)} custom-call(bf16[1024,3072]{1,0:T(8,128)(2,1)} %get-tuple-element.82.a, bf16[1024,768]{1,0:T(8,128)(2,1)} %b.1), custom_call_target="tpu_custom_call" | custom-call | tf_op jit(solution)/shard_map/outer_rows/pallas_call | solution.py:358
  131.7 4.3 %outer_cols.3.gout_h = bf16[768,768]{1,0:T(8,128)(2,1)} custom-call(bf16[1024,768]{1,0:T(8,128)(2,1)} %get-tuple-element.65.mix.a, bf16[1024,768]{1,0:T(8,128)(2,1)} %get-tuple-element.85.b), custom_call_target="tpu_custom_call" | custom-call | tf_op jit(solution)/shard_map/outer_cols/pallas_call | solution.py:372
  136.0 10.3 %outer_cols.2.gup_h = bf16[768,3072]{1,0:T(8,128)(2,1)} custom-call(bf16[1024,768]{1,0:T(8,128)(2,1)} %get-tuple-element.83.a, bf16[1024,3072]{1,0:T(8,128)(2,1)} %get-tuple-element.84.b), custom_call_target="tpu_custom_call" | custom-call | tf_op jit(solution)/shard_map/outer_cols/pallas_call | solution.py:372
  146.3 0.0 copy-start.2
  146.4 0.0 copy-start.4
  146.4 0.0 copy-start.5
  146.4 0.0 copy-start.3
  146.4 0.0 copy-start.6
  146.4 0.0 copy-start.7
  146.4 147.8 %attend_reduce.1 = (bf16[2304,768]{1,0:T(8,128)(2,1)}, f32[1024,768]{1,0:T(8,128)}, f32[8,128]{1,0:T(8,128)}, f32[16,768]{1,0:T(8,128)}) custom-call(s32[1]{0:T(128)S(6)} %copy.51.block_shift, f32[24,1024]{1,0:T(8,128)} %get-tuple-element.61.lse, f32[24,1024]{1,0:T(8,128)} %get-tuple-element.69.delta, f32[1024,128]{1,0:T(8,128)} %constant.19.clone.cos, ...), custom_call_target="tpu_custom_call" | custom-call | tf_op jit(solution)/shard_map/attend_reduce/pallas_call | solution.py:1281
  294.2 1.2 slice.11
  296.1 0.8 multiply_reduce_fusion
  296.9 1.4 multiply_subtract_fusion
  298.3 0.6 multiply_subtract_fusion.1
  298.9 3.9 %adam.5 = (f32[192,768]{1,0:T(8,128)}, f32[192,768]{1,0:T(8,128)}, f32[192,768]{1,0:T(8,128)}) custom-call(f32[1]{0:T(128)} %bitcast.1.norm, f32[192,768]{1,0:T(8,128)} %w.5, f32[192,768]{1,0:T(8,128)} %m.5, f32[192,768]{1,0:T(8,128)} %s.5, bf16[2304,768]{1,0:T(8,128)(2,1)} %get-tuple-element.88.g), custom_call_target="tpu_custom_call" | custom-call | tf_op jit(solution)/shard_map/adam/pallas_call | solution.py:1341
  302.8 10.0 %adam.4 = (f32[192,2304]{1,0:T(8,128)}, f32[192,2304]{1,0:T(8,128)}, f32[192,2304]{1,0:T(8,128)}) custom-call(f32[1]{0:T(128)} %bitcast.1.norm, f32[192,2304]{1,0:T(8,128)} %w.4, f32[192,2304]{1,0:T(8,128)} %m.4, f32[192,2304]{1,0:T(8,128)} %s.4, bf16[2304,768]{1,0:T(8,128)(2,1)} %get-tuple-element.88.g), custom_call_target="tpu_custom_call" | custom-call | tf_op jit(solution)/shard_map/adam/pallas_call | solution.py:1341
  312.8 8.7 %adam.7 = (f32[768,768]{1,0:T(8,128)}, f32[768,768]{1,0:T(8,128)}, f32[768,768]{1,0:T(8,128)}) custom-call(f32[1]{0:T(128)} %bitcast.1.norm, f32[768,768]{1,0:T(8,128)} %w.7, f32[768,768]{1,0:T(8,128)} %m.7, f32[768,768]{1,0:T(8,128)} %s.7, bf16[2304,768]{1,0:T(8,128)(2,1)} %get-tuple-element.88.g), custom_call_target="tpu_custom_call" | custom-call | tf_op jit(solution)/shard_map/adam/pallas_call | solution.py:1341
  321.6 8.6 %adam.6 = (f32[192,3072]{1,0:T(8,128)}, f32[192,3072]{1,0:T(8,128)}, f32[192,3072]{1,0:T(8,128)}) custom-call(f32[1]{0:T(128)} %bitcast.1.norm, f32[192,3072]{1,0:T(8,128)} %w.6, f32[192,3072]{1,0:T(8,128)} %m.6, f32[192,3072]{1,0:T(8,128)} %s.6, bf16[2304,768]{1,0:T(8,128)(2,1)} %get-tuple-element.88.g), custom_call_target="tpu_custom_call" | custom-call | tf_op jit(solution)/shard_map/adam/pallas_call | solution.py:1341
  330.1 1.7 copy.52
  (11 shorter events, 0.0 us)
Async XLA Ops:
  3.8 1.0 copy-start.1
  146.3 150.5 %copy-start.2 = (f32[6,192]{1,0:T(8,128)S(1)}, f32[6,192]{1,0:T(8,128)}, u32[]{:S(2)}) copy-start(f32[6,192]{1,0:T(8,128)} %param.43) | copy-start | bytes 13828
  146.4 150.5 %copy-start.4 = (f32[6,192]{1,0:T(8,128)S(1)}, f32[6,192]{1,0:T(8,128)}, u32[]{:S(2)}) copy-start(f32[6,192]{1,0:T(8,128)} %param.45) | copy-start | bytes 13828
  146.4 150.5 %copy-start.5 = (f32[6,192]{1,0:T(8,128)S(1)}, f32[6,192]{1,0:T(8,128)}, u32[]{:S(2)}) copy-start(f32[6,192]{1,0:T(8,128)} %param.44) | copy-start | bytes 13828
  146.4 151.9 %copy-start.3 = (f32[768]{0:T(1024)S(1)}, f32[768]{0:T(1024)}, u32[]{:S(2)}) copy-start(f32[768]{0:T(1024)} %param.40) | copy-start | bytes 9220
  146.4 151.9 %copy-start.6 = (f32[768]{0:T(1024)S(1)}, f32[768]{0:T(1024)}, u32[]{:S(2)}) copy-start(f32[768]{0:T(1024)} %param.42) | copy-start | bytes 9220
  146.4 151.9 %copy-start.7 = (f32[768]{0:T(1024)S(1)}, f32[768]{0:T(1024)}, u32[]{:S(2)}) copy-start(f32[768]{0:T(1024)} %param.41) | copy-start | bytes 9220
  321.5 8.6 %copy-start = (f32[1024,768]{1,0:T(8,128)S(1)}, f32[1024,768]{1,0:T(8,128)}, u32[]{:S(2)}) copy-start(f32[1024,768]{1,0:T(8,128)} %get-tuple-element.129) | copy-start | bytes 9437188
